TPU v7x, 256 devices: a whole 4x4x8 slice. The times are simulated.
256 devices in a mesh: dp: 16 (over y, x), leaf: 16 (over z, core).
Axes of the slice: x: 4, y: 4, z: 8, core: 2. Of those that a mesh axis runs over, the one named last changes fastest.
Arguments:
- audio_feats: bfloat16 [49152, 27, 512], P(('dp', 'leaf')), may hold values from -24 to 24
- conv_weight: bfloat16 [2, 3, 512, 512], replicated, may hold values from -0.15625 to 0.15625
- head_weight: bfloat16 [32768, 512], P('leaf'), may hold values from -0.25 to 0.25
- clip_owner: int32 [49152, 2], P(('dp', 'leaf')), may hold values from 0 to 15, all different within a row; in each aligned block of 192 rows (0 to 191, 192 to 383, ...) at most 48 rows name the same one
- node_ids: int32 [49152, 2, 8], P(('dp', 'leaf')), may hold values from 0 to 2047
Outputs:
- conv_grad: bfloat16 [2, 3, 512, 512], P(None, None, 'dp', 'leaf')
- head_grad: bfloat16 [32768, 512], P(('leaf', 'dp'))
Inputs may be any that keep to these rules, and one draw needn't show every extreme that they name: `clip_owner`: each clip names 2 different owners; among the 192 clips of one device (aligned blocks of rows) no owner is named more than 48 times. `node_ids`: node indices are local to the owner named by the same route.
All inputs are finite; a program needn't handle non-finite values.
Results may differ from a plain program's by a relative error of at most 0.011.
Values may be sent and summed in bfloat16 or wider, within the bound.
A program may use at most 128 MiB of HBM per device.

v0:
```python
import jax
import jax.numpy as jnp
from jax import lax
from jax.sharding import PartitionSpec as P

inv_root_two = 0.7071067811865476
inv_root_two_pi = 0.3989422804014327


def gelu_value(value):
    return 0.5 * value * (1.0 + lax.erf(value * inv_root_two))


def gelu_slope(value):
    return (
        0.5 * (1.0 + lax.erf(value * inv_root_two))
        + value * jnp.exp(-0.5 * value * value) * inv_root_two_pi
    )


def score_routes(slot_emb, slot_nodes, usable, head_weight, labels):
    rows_bf = head_weight[slot_nodes]
    logits = jnp.einsum("spc,sc->sp", rows_bf, slot_emb, preferred_element_type=jnp.float32)
    dlogit = jnp.where(usable, jax.nn.sigmoid(logits) - labels, 0.0)
    route_grad = jnp.einsum(
        "sp,spc->sc", dlogit, rows_bf.astype(jnp.float32), precision=lax.Precision.HIGHEST
    ).astype(jnp.bfloat16)
    terms = dlogit[:, :, None] * slot_emb.astype(jnp.float32)[:, None, :]
    head_local = jax.ops.segment_sum(
        terms.reshape(-1, slot_emb.shape[1]),
        slot_nodes.reshape(-1),
        num_segments=head_weight.shape[0],
    )
    return (route_grad, head_local)


def body(audio_feats, conv_weight, head_weight, clip_owner, node_ids):
    clip_count = audio_feats.shape[0]
    channels = audio_feats.shape[2]
    layer_count = conv_weight.shape[0]
    route_count = clip_owner.shape[1]
    pair_count = node_ids.shape[2]
    owner_count = lax.axis_size("leaf")
    capacity = 2 * clip_count * route_count // owner_count
    activation = audio_feats
    layer_inputs = []
    pre_list = []
    for layer_index in range(layer_count):
        length = activation.shape[1] // 3
        folded = activation.reshape(clip_count * length, 3 * channels)
        pre_act = jnp.dot(
            folded,
            conv_weight[layer_index].reshape(3 * channels, channels),
            preferred_element_type=jnp.float32,
        )
        layer_inputs.append(folded)
        pre_list.append(pre_act)
        if layer_index + 1 < layer_count:
            activation = (
                gelu_value(pre_act).astype(jnp.bfloat16).reshape(clip_count, length, channels)
            )
    final_pre = pre_list[-1].reshape(clip_count, 3, channels)
    embedding = jnp.mean(gelu_value(final_pre), axis=1).astype(jnp.bfloat16)
    labels = (jnp.arange(pair_count) < pair_count // 2).astype(jnp.float32)
    flat_owner = clip_owner.reshape(-1)
    owner_hits = (flat_owner[:, None] == jnp.arange(owner_count, dtype=jnp.int32)[None, :]).astype(
        jnp.int32
    )
    running = jnp.cumsum(owner_hits, axis=0) - 1
    slot_index = jnp.sum(running * owner_hits, axis=1)
    position = flat_owner * capacity + slot_index
    repeated = jnp.repeat(embedding, route_count, axis=0)
    send_emb = (
        jnp.zeros((owner_count * capacity, channels), jnp.bfloat16).at[position].set(repeated)
    )
    send_nodes = (
        jnp.full((owner_count * capacity, pair_count), -1, jnp.int32)
        .at[position]
        .set(node_ids.reshape(-1, pair_count))
    )
    got_emb, got_nodes = (
        lax.all_to_all(
            send_emb.reshape(owner_count, capacity, channels),
            "leaf",
            split_axis=0,
            concat_axis=0,
            tiled=True,
        ),
        lax.all_to_all(
            send_nodes.reshape(owner_count, capacity, pair_count),
            "leaf",
            split_axis=0,
            concat_axis=0,
            tiled=True,
        ),
    )
    got_emb = got_emb.reshape(-1, channels)
    got_nodes = got_nodes.reshape(-1, pair_count)
    usable = got_nodes >= 0
    local_node = jnp.maximum(got_nodes, 0)
    route_grad, head_local = score_routes(got_emb, local_node, usable, head_weight, labels)
    returned = lax.all_to_all(
        route_grad.reshape(owner_count, capacity, channels),
        "leaf",
        split_axis=0,
        concat_axis=0,
        tiled=True,
    )
    picked = returned.reshape(-1, channels)[position].astype(jnp.float32)
    clip_grad = jnp.sum(picked.reshape(clip_count, route_count, channels), axis=1)
    head_grad = lax.psum_scatter(head_local, "dp", scatter_dimension=0, tiled=True).astype(
        jnp.bfloat16
    )
    upstream = (
        (clip_grad[:, None, :] / 3.0 * gelu_slope(final_pre))
        .astype(jnp.bfloat16)
        .reshape(clip_count * 3, channels)
    )
    grad_list = []
    for layer_index in range(layer_count - 1, -1, -1):
        weight_flat = conv_weight[layer_index].reshape(3 * channels, channels)
        layer_term = lax.dot_general(
            layer_inputs[layer_index],
            upstream,
            (((0,), (0,)), ((), ())),
            preferred_element_type=jnp.float32,
        )
        grad_list = [layer_term] + grad_list
        if layer_index > 0:
            back_prop = lax.dot_general(
                upstream, weight_flat, (((1,), (1,)), ((), ())), preferred_element_type=jnp.float32
            )
            back_prop = back_prop.reshape(-1, channels)
            upstream = (back_prop * gelu_slope(pre_list[layer_index - 1])).astype(jnp.bfloat16)
    local_grad = jnp.stack(grad_list).reshape(layer_count, 3, channels, channels)
    section_one = lax.psum_scatter(local_grad, "dp", scatter_dimension=2, tiled=True)
    conv_grad = lax.psum_scatter(section_one, "leaf", scatter_dimension=3, tiled=True)
    return (conv_grad.astype(jnp.bfloat16), head_grad)


def solution(mesh):
    placed = (
        P(("dp", "leaf"), None, None),
        P(),
        P("leaf", None),
        P(("dp", "leaf"), None),
        P(("dp", "leaf"), None, None),
    )
    return jax.shard_map(
        body,
        mesh=mesh,
        in_specs=placed,
        out_specs=(P(None, None, "dp", "leaf"), P(("leaf", "dp"), None)),
        check_vma=False,
    )
```

profile of v0, /device:TPU:1, one launch (start us, length us, event | category | flops | bytes accessed | tf_op | source)
XLA Modules:
  0.0 409.6 jit_solution(4048472804713347604)
XLA Ops:
  11.5 1.5 scatter_custom_fusion
  13.9 10.0 %all-to-all-start = ((s32[16,1,384]{2,1,0:T(1,128)}), s32[16,1,384]{2,1,0:T(1,128)S(1)}, u32[]{:S(2)}, u32[]{:S(2)}) async-start(s32[16,1,384]{2,1,0:T(1,128)} %reshape.219), calls=%async_computation | async-start | bytes 49152 | tf_op jit(solution)/shard_map/all_to_all | solution.py:89
  23.9 8.3 %copy.56 = bf16[192,27,512]{2,1,0:T(8,128)(2,1)} copy(bf16[192,27,512]{2,0,1:T(8,128)(2,1)} %param.5) | data formatting | bytes 10616832 | tf_op args[0]
  32.2 8.6 %reshape.149 = bf16[1728,1536]{1,0:T(8,128)(2,1)} reshape(bf16[192,27,512]{2,1,0:T(8,128)(2,1)} %copy.56) | data formatting | bytes 10616832 | tf_op jit(solution)/shard_map/reshape | solution.py:50
  40.8 3.4 fusion.43
  44.9 4.7 %multiply_convert_fusion = (bf16[1728,512]{1,0:T(8,128)(2,1)}, f32[1728,512]{1,0:T(8,128)}) fusion(bf16[1728,1536]{1,0:T(8,128)(2,1)S(1)} %copy-done.3, bf16[1536,512]{1,0:T(8,128)(2,1)S(1)} %bitcast.87), kind=kOutput, calls=%fused_computation.21 | convolution fusion | flops 2722332672 | bytes 12189696 | tf_op jit(solution)/shard_map/dot_general | solution.py:51
  49.6 5.2 %dot_general.30 = bf16[192,3,1536]{2,1,0:T(4,128)(2,1)} reshape(bf16[1728,512]{1,0:T(8,128)(2,1)} %get-tuple-element.4) | data formatting | bytes 3538944 | tf_op jit(solution)/shard_map/dot_general | solution.py:51
  54.7 4.3 %multiply_reduce_fusion = (f32[192,512]{1,0:T(8,128)S(1)}, f32[192,3,512]{2,0,1:T(8,128)}) fusion(bf16[1536,512,1]{1,0,2:T(8,128)(2,1)} %bitcast.85, bf16[192,3,1536]{2,1,0:T(4,128)(2,1)} %dot_general.30), kind=kOutput, calls=%fused_computation.40 | convolution fusion | flops 907345920 | bytes 4915200 | tf_op jit(solution)/shard_map/dot_general | solution.py:51
  59.5 2.9 scatter_custom_fusion.1
  62.4 7.2 %all-to-all-start.1 = ((bf16[16,48,512]{2,1,0:T(8,128)(2,1)}), bf16[16,48,512]{2,1,0:T(8,128)(2,1)S(1)}, u32[]{:S(2)}, u32[]{:S(2)}) async-start(bf16[16,48,512]{2,1,0:T(8,128)(2,1)} %bitcast.7), calls=%async_computation.1 | async-start | bytes 1572864 | tf_op jit(solution)/shard_map/all_to_all | solution.py:82
  71.5 25.4 %gather_fusion = bf16[6144,512]{1,0:T(8,128)(2,1)} fusion(bf16[2048,512]{1,0:T(8,128)(2,1)S(1)} %copy-done, s32[6144]{0:T(1024)S(1)} %broadcast_clamp_fusion), kind=kCustom, calls=%fused_computation | custom fusion | bytes 12607488 | tf_op jit(solution)/shard_map/gather | solution.py:22
  96.9 5.5 %fusion.1 = f32[768,1,8]{2,1,0:T(1,128)S(1)} fusion(bf16[6144,512]{1,0:T(8,128)(2,1)} %gather_fusion, bf16[768,512,1]{1,0,2:T(8,128)(2,1)S(1)} %bitcast.81), kind=kOutput, calls=%fused_computation.8 | convolution fusion | flops 6291456 | bytes 7102464 | tf_op jit(solution)/shard_map/spc,sc->sp/dot_general | solution.py:23
  103.1 7.5 %fusion.3 = bf16[768,1,512]{2,1,0:T(2,128)(2,1)S(1)} fusion(f32[768,8,1]{1,2,0:T(1,128)S(1)} %copy.65, bf16[6144,512]{1,0:T(8,128)(2,1)} %gather_fusion), kind=kOutput, calls=%fused_computation.10 | convolution fusion | flops 37748736 | bytes 7102464 | tf_op jit(solution)/shard_map/sp,spc->sc/dot_general | solution.py:25
  111.7 7.2 %all-to-all-start.2 = ((bf16[16,48,512]{2,1,0:T(8,128)(2,1)}), bf16[16,48,512]{2,1,0:T(8,128)(2,1)S(1)}, u32[]{:S(2)}, u32[]{:S(2)}) async-start(bf16[16,48,512]{2,1,0:T(8,128)(2,1)} %bitcast.82), calls=%async_computation.2 | async-start | bytes 1572864 | tf_op jit(solution)/shard_map/all_to_all | solution.py:102
  119.2 3.9 reshape_reshape.3
  123.1 3.9 copy.60
  126.9 14.6 %all-to-all-done.2 = bf16[16,48,512]{2,1,0:T(8,128)(2,1)S(1)} async-done(((bf16[16,48,512]{2,1,0:T(8,128)(2,1)}), bf16[16,48,512]{2,1,0:T(8,128)(2,1)S(1)}, u32[]{:S(2)}, u32[]{:S(2)}) %all-to-all-start.2) | async-done | bytes 786464 | tf_op jit(solution)/shard_map/all_to_all | solution.py:102
  141.6 2.1 gather_fusion.1
  145.1 1.8 fusion.26
  148.5 4.3 %fusion.44 = f32[576,1536]{1,0:T(8,128)} fusion(bf16[576,512]{1,0:T(8,128)(2,1)S(1)} %reshape.155, bf16[1536,512]{1,0:T(8,128)(2,1)} %bitcast.86), kind=kOutput, calls=%fused_computation.75 | convolution fusion | flops 905969664 | bytes 5701632 | tf_op jit(solution)/shard_map/dot_general | solution.py:130
  152.8 4.8 %reshape.156 = f32[1728,512]{1,0:T(8,128)} reshape(f32[576,1536]{1,0:T(8,128)} %fusion.44) | data formatting | bytes 7077888 | tf_op jit(solution)/shard_map/reshape | solution.py:133
  157.6 9.8 %convolution_bitcast_fusion = f32[1536,512]{0,1:T(8,128)} fusion(bf16[1728,1536]{1,0:T(8,128)(2,1)} %reshape.149, f32[1728,512]{1,0:T(8,128)} %reshape.156, f32[1728,512]{1,0:T(8,128)} %get-tuple-element.5), kind=kOutput, calls=%fused_computation.23 | convolution fusion | flops 2726756352 | bytes 15532032 | tf_op jit(solution)/shard_map/dot_general | solution.py:122
  167.4 3.7 copy.59
  171.1 1.4 convolution_bitcast_fusion.1
  173.0 3.4 pad_maximum_fusion
  177.4 45.2 %scatter_custom_fusion.2 = f32[2048,512]{1,0:T(8,128)} fusion(s32[6144]{0:T(1024)S(1)} %reshape.161, f32[768,512]{1,0:T(8,128)S(1)} %bitcast_convert_fusion.1, f32[6144]{0:T(1024)S(1)} %mul.137, f32[]{:T(128)} %constant.21.clone.1), kind=kCustom, calls=%fused_computation.6 | custom fusion | flops 6291456 | bytes 5791748 | tf_op jit(solution)/shard_map/scatter-add | solution.py:29
  222.7 36.2 %reduce-scatter.6.cloned.1.call-done = f32[2,3,32,512]{3,2,1,0:T(8,128)} async-done(((f32[2,3,512,512]{3,2,1,0:T(8,128)}), f32[2,3,32,512]{3,2,1,0:T(8,128)}) %reduce-scatter.6.cloned.1.call-update) | async-done | bytes 393232 | tf_op jit(solution)/shard_map/reduce_scatter | solution.py:136
  258.9 2.6 copy.70
  261.6 3.5 reshape.209
  265.1 79.0 %reduce-scatter.8.cloned.1.call-done = f32[128,512]{1,0:T(8,128)} async-done(((f32[2048,512]{1,0:T(8,128)}), f32[128,512]{1,0:T(8,128)}) %reduce-scatter.8.cloned.1.call-update) | async-done | bytes 262160 | tf_op jit(solution)/shard_map/reduce_scatter | solution.py:111
  344.1 1.6 convert_element_type.59
  345.7 55.8 %reduce-scatter.10.cloned.1.call-done = f32[32,192]{1,0:T(8,128)} async-done(((f32[512,192]{1,0:T(8,128)}), f32[32,192]{1,0:T(8,128)}) %reduce-scatter.10.cloned.1.call-update) | async-done | bytes 24592
  (63 shorter events, 16.1 us)
Async XLA Ops:
  7.2 64.3 %copy-start = (bf16[2048,512]{1,0:T(8,128)(2,1)S(1)}, bf16[2048,512]{1,0:T(8,128)(2,1)}, u32[]{:S(2)}) copy-start(bf16[2048,512]{1,0:T(8,128)(2,1)} %param.7) | copy-start | bytes 6291460
  13.9 48.5 %all-to-all-start = ((s32[16,1,384]{2,1,0:T(1,128)}), s32[16,1,384]{2,1,0:T(1,128)S(1)}, u32[]{:S(2)}, u32[]{:S(2)}) async-start(s32[16,1,384]{2,1,0:T(1,128)} %reshape.219), calls=%async_computation | async-start | bytes 49152 | tf_op jit(solution)/shard_map/all_to_all | solution.py:89
  40.8 4.0 copy-start.3
  62.4 34.5 %all-to-all-start.1 = ((bf16[16,48,512]{2,1,0:T(8,128)(2,1)}), bf16[16,48,512]{2,1,0:T(8,128)(2,1)S(1)}, u32[]{:S(2)}, u32[]{:S(2)}) async-start(bf16[16,48,512]{2,1,0:T(8,128)(2,1)} %bitcast.7), calls=%async_computation.1 | async-start | bytes 1572864 | tf_op jit(solution)/shard_map/all_to_all | solution.py:82
  111.7 29.9 %all-to-all-start.2 = ((bf16[16,48,512]{2,1,0:T(8,128)(2,1)}), bf16[16,48,512]{2,1,0:T(8,128)(2,1)S(1)}, u32[]{:S(2)}, u32[]{:S(2)}) async-start(bf16[16,48,512]{2,1,0:T(8,128)(2,1)} %bitcast.82), calls=%async_computation.2 | async-start | bytes 1572864 | tf_op jit(solution)/shard_map/all_to_all | solution.py:102
  118.9 140.0 %reduce-scatter.6.cloned.1.call-start = ((), (), s32[]{:S(2)}) async-start(), calls=%async_computation.6 | async-start | bytes 6684672 | tf_op jit(solution)/shard_map/reduce_scatter | solution.py:136
  167.4 3.7 copy-start.4
  171.1 1.9 copy-start.2
  176.5 167.6 %reduce-scatter.8.cloned.1.call-start = ((), (), s32[]{:S(2)}) async-start(), calls=%async_computation.7 | async-start | bytes 4456448 | tf_op jit(solution)/shard_map/reduce_scatter | solution.py:111
  222.6 180.4 %copy-start.1 = (bf16[2048,512]{1,0:T(8,128)(2,1)S(1)}, bf16[2048,512]{1,0:T(8,128)(2,1)}, u32[]{:S(2)}) copy-start(bf16[2048,512]{1,0:T(8,128)(2,1)} %param.7) | copy-start | bytes 6291460
  222.7 178.8 %reduce-scatter.10.cloned.1.call-start = ((), (), s32[]{:S(2)}) async-start(), calls=%async_computation.8 | async-start | bytes 557056
Sparse Core Ops, SparseCore 0:
  176.6 82.3 reduce-scatter.5
  262.6 81.4 reduce-scatter.7
  346.7 54.7 reduce-scatter.9
where the time goes:
time: 413 us; the launch traced here: 410 us
  waiting for transfers between devices  186 us (45%)
  local copies, waits for them, and re-layouts  91.5 us (22%)
  other arithmetic  55.8 us (14%)
  matrix products  37.6 us (9%)
  starting transfers between devices  25 us (6%)
  between operations  14 us (3%)
    reduce_scatter x1, waiting for transfers between devices, body(): lax.psum_scatter(head_local, 'dp', scatter_dimension=0, tiled=True)  79 us
    unnamed x4, waiting for transfers between devices  55.8 us
    scatter-add x1, other arithmetic, score_routes(): jax.ops.segment_sum(terms.reshape(-1, slot_emb.shape[1]), slot_nodes.resh...  45.2 us
    reduce_scatter x1, waiting for transfers between devices, body(): lax.psum_scatter(local_grad, 'dp', scatter_dimension=2, tiled=True)  36.2 us
    gather x1, local copies, waits for them, and re-layouts, score_routes(): rows_bf = head_weight[slot_nodes]  25.4 us
    unnamed x19, local copies, waits for them, and re-layouts  19.7 us
    all_to_all x1, waiting for transfers between devices, body(): lax.all_to_all(route_grad.reshape(owner_count, capacity, channels), 'leaf...  14.6 us
    dot_general x2, matrix products, body(): lax.dot_general(layer_inputs[layer_index], upstream, (((0,), (0,)), ((),...  11.2 us
  transfers between devices with their start and end apart: 6, of which 4 were waited for; matrix products, arithmetic and copies ran while one was open for 31% of the time, Pallas kernels for 0%

commit v1 on v0

v1 whole, which is shorter than its diff:
```python
import functools

import jax
import jax.numpy as jnp
from jax import lax
from jax.experimental import pallas as pl
from jax.experimental.pallas import tpu as pltpu
from jax.sharding import PartitionSpec as P

MESH = pl.DeviceIdType.MESH
F32 = jnp.float32
BF16 = jnp.bfloat16
INV_ROOT_TWO = 0.7071067811865476
INV_ROOT_TWO_PI = 0.3989422804014327

NT = (((1,), (1,)), ((), ()))
TN = (((0,), (0,)), ((), ()))


def dot(a, b, dims=(((1,), (0,)), ((), ()))):
    return lax.dot_general(a, b, dims, preferred_element_type=F32)


def gelu_pair(value):
    half = 0.5 * (1.0 + lax.erf(value * INV_ROOT_TWO))
    bell = jnp.exp(-0.5 * value * value) * INV_ROOT_TWO_PI
    return value * half, half + value * bell


def bytes_wait(ref, sem):
    pltpu.make_async_copy(ref, ref, sem).wait()


def kernel(
    nd, nl, chunk, groups,
    a_hbm, w_hbm, h_hbm, own_ref, node_ref,
    conv_ref, head_ref,
    a_v, w_v, h_v, ht_v, p_v, a1_v, sl0_v, sl1_v, emb_v, d_v,
    nsend_v, nrecv_v, esend_v, erecv_v, call_v, cpos_v, st_v, gsend_v, grecv_v,
    hsend_v, hrecv_v, u1_v, u0_v, wown_v, wsend_v, wrecv_v, dsend_v, drecv_v,
    g_v, zsend_v, zrecv_v, zsum_v,
    load_sem, a_sem, n_sem, e_sem, erecv_sem, g_sem, h_sem, csend_sem, crecv_sem,
    dsend_sem, drecv_sem, zsend_sem, zrecv_sem,
):
    me = lax.axis_index("leaf")
    mine = lax.axis_index("dp")
    core = lax.rem(me, 2)
    sibling = me + 1 - 2 * core
    clips = emb_v.shape[0]
    chan = emb_v.shape[1]
    cap = esend_v.shape[0] // nl
    slots = nl * cap
    nodes = h_v.shape[0]
    pairs = node_ref.shape[1]
    half = chan // 2
    span = nodes // nd
    rows_dp = chan // nd
    cols_leaf = chan // nl
    steps = clips // chunk

    load_w0 = pltpu.make_async_copy(w_hbm.at[0], w_v.at[0], load_sem.at[0])
    load_w1 = pltpu.make_async_copy(w_hbm.at[1], w_v.at[1], load_sem.at[1])
    load_h = pltpu.make_async_copy(h_hbm, h_v, load_sem.at[2])

    def load_a(i):
        part = pl.ds(pl.multiple_of(i * chunk, chunk), chunk)
        return pltpu.make_async_copy(a_hbm.at[:, :, part], a_v.at[:, :, part], a_sem.at[i])

    load_w0.start()
    for i in range(steps):
        load_a(i).start()
    load_w1.start()
    load_h.start()

    barrier = pltpu.get_barrier_semaphore()

    @pl.loop(1, nl)
    def _(i):
        pl.semaphore_signal(
            barrier, inc=1, device_id={"leaf": lax.rem(me + i, nl)}, device_id_type=MESH
        )

    @pl.loop(1, nd)
    def _(i):
        pl.semaphore_signal(
            barrier, inc=1, device_id={"dp": lax.rem(mine + i, nd)}, device_id_type=MESH
        )

    owner_iota = lax.broadcasted_iota(jnp.int32, (nl, clips), 0)
    before = (
        lax.broadcasted_iota(jnp.int32, (clips, clips), 0)
        < lax.broadcasted_iota(jnp.int32, (clips, clips), 1)
    ).astype(F32).astype(BF16)
    slot_iota = lax.broadcasted_iota(jnp.int32, (slots, clips), 0)
    base = jnp.zeros((nl, 1), F32)
    spots = []
    lists = jnp.zeros((slots, 128), F32)
    for r in range(2):
        hit = (own_ref[r : r + 1, :] == owner_iota).astype(F32)
        rank = dot(hit.astype(BF16), before) + base
        base = base + jnp.sum(hit, axis=1, keepdims=True)
        place = jnp.sum(hit * (rank + (owner_iota * cap).astype(F32)), axis=0, keepdims=True)
        spot = (slot_iota == place.astype(jnp.int32)).astype(F32).astype(BF16)
        spots.append(spot)
        ident = node_ref[r] + 1
        upper = (ident >> 7).astype(F32)
        lower = (ident & 127).astype(F32)
        pad = jnp.zeros((128 - pairs, clips), F32)
        upper = jnp.concatenate([upper, pad], axis=0).astype(BF16)
        lower = jnp.concatenate([lower, pad], axis=0).astype(BF16)
        lists = lists + dot(spot, upper, NT) * 128.0 + dot(spot, lower, NT)
    d_v[...] = spots[0] + spots[1]
    nsend_v[...] = lists - 1.0

    pl.semaphore_wait(barrier, nl - 1 + nd - 1)

    def block(i):
        return pl.ds(pl.multiple_of(i * cap, cap), cap)

    per = nl // groups
    group = me // per
    inside = lax.rem(me, per)

    def peers(t):
        if t == 0:
            return [group * per + lax.rem(inside + o, per) for o in range(1, per)]
        return [lax.rem(group + t, groups) * per + o for o in range(per)]

    nrecv_v[block(me), :] = nsend_v[block(me), :]

    @pl.loop(1, nl)
    def _(i):
        to = lax.rem(me + i, nl)
        pltpu.make_async_remote_copy(
            nsend_v.at[block(to)], nrecv_v.at[block(me)], n_sem.at[0], n_sem.at[1],
            device_id={"leaf": to}, device_id_type=MESH,
        ).start()

    load_w0.wait()

    @pl.loop(0, steps)
    def _(i):
        load_a(i).wait()
        part = pl.ds(pl.multiple_of(i * chunk, chunk), chunk)
        folded = jnp.concatenate(
            [a_v[:, k, part, :].reshape(9 * chunk, chan) for k in range(3)], axis=1
        )
        p_v[...] = dot(folded, w_v[0]).reshape(9, chunk, chan)

        @pl.loop(0, 9)
        def _(j):
            act, slope = gelu_pair(p_v[j])
            a1_v[j, part, :] = act.astype(BF16)
            sl0_v[j, part, :] = slope

    load_w1.wait()

    @pl.loop(0, 3)
    def _(j):
        folded = jnp.concatenate([a1_v[3 * j + k] for k in range(3)], axis=1)
        sl1_v[j] = dot(folded, w_v[1])

    @pl.loop(0, steps)
    def _(i):
        part = pl.ds(pl.multiple_of(i * chunk, chunk), chunk)
        total = jnp.zeros((chunk, chan), F32)
        for j in range(3):
            act, slope = gelu_pair(sl1_v[j, part, :])
            sl1_v[j, part, :] = slope
            total = total + act
        emb_v[part, :] = (total * (1.0 / 3.0)).astype(BF16)

    esend_v[...] = dot(d_v[...], emb_v[...]).astype(BF16)
    erecv_v[block(me), :] = esend_v[block(me), :]

    def emb_copy(to, source):
        return pltpu.make_async_remote_copy(
            esend_v.at[block(to)], erecv_v.at[block(source)], e_sem.at[0],
            erecv_sem.at[source], device_id={"leaf": to}, device_id_type=MESH,
        )

    for t in range(groups):
        for to in peers(t):
            emb_copy(to, me).start()

    load_h.wait()
    piece = nodes // 4

    for i in range(4):
        ht_v[:, i * piece : (i + 1) * piece] = h_v[i * piece : (i + 1) * piece, :].T

    bytes_wait(nsend_v.at[pl.ds(0, (nl - 1) * cap)], n_sem.at[0])
    bytes_wait(nrecv_v.at[pl.ds(0, (nl - 1) * cap)], n_sem.at[1])
    node_iota = lax.broadcasted_iota(jnp.int32, (16, nodes), 1).astype(F32)

    @pl.loop(0, slots // 16)
    def _(i):
        part = pl.ds(pl.multiple_of(i * 16, 16), 16)
        named = nrecv_v[part, :]
        tally = jnp.zeros((16, nodes), F32)
        for q in range(pairs):
            weight = 17.0 if q < pairs // 2 else 1.0
            tally = tally + jnp.where(named[:, q : q + 1] == node_iota, weight, 0.0)
        positive = jnp.floor(tally * (1.0 / 16.0))
        cpos_v[part, :] = positive.astype(BF16)
        call_v[part, :] = (tally - 16.0 * positive).astype(BF16)

    lanes = nodes // 4
    for t in range(groups):
        source_group = lax.rem(group + groups - t, groups)
        for i in range(per):
            source = source_group * per + i
            if t == 0:

                @pl.when(source != me)
                def _():
                    emb_copy(source, source).wait_recv()
            else:
                emb_copy(source, source).wait_recv()
        start = pl.multiple_of(source_group * (per * cap), per * cap)
        rows = pl.ds(start, per * cap)
        emb = erecv_v[rows, :]

        @pl.loop(0, 4)
        def _(n):
            cols = pl.ds(pl.multiple_of(n * lanes, lanes), lanes)
            score = dot(emb, ht_v[:, cols])
            sig = 0.5 * jnp.tanh(0.5 * score) + 0.5
            st_v[rows, cols] = (
                sig * call_v[rows, cols].astype(F32) - cpos_v[rows, cols].astype(F32)
            ).astype(BF16)

        gsend_v[rows, :] = dot(st_v[rows, :], h_v[...]).astype(BF16)
        if t == 0:
            grecv_v[block(me), :] = gsend_v[block(me), :]
            back = [group * per + lax.rem(inside + o, per) for o in range(1, per)]
        else:
            back = [source_group * per + o for o in range(per)]
        for to in back:
            pltpu.make_async_remote_copy(
                gsend_v.at[block(to)], grecv_v.at[block(me)], g_sem.at[0], g_sem.at[1],
                device_id={"leaf": to}, device_id_type=MESH,
            ).start()

    @pl.loop(0, nd)
    def _(i):
        to = lax.rem(mine + i, nd)
        cols = pl.ds(pl.multiple_of(to * span, span), span)
        hsend_v[to] = dot(st_v[:, cols], erecv_v[...], TN).astype(BF16)

        @pl.when(i > 0)
        def _():
            pltpu.make_async_remote_copy(
                hsend_v.at[to], hrecv_v.at[mine], h_sem.at[0], h_sem.at[1],
                device_id={"dp": to}, device_id_type=MESH,
            ).start()

    hrecv_v[mine] = hsend_v[mine]

    bytes_wait(grecv_v.at[pl.ds(0, (nl - 1) * cap)], g_sem.at[1])
    clip_grad = dot(d_v[...], grecv_v[...], TN) * (1.0 / 3.0)
    for j in range(3):
        u1_v[j] = (clip_grad * sl1_v[j]).astype(BF16)

    def leave(step, grad):
        low, high = grad[:, :half], grad[:, half:]
        wown_v[step] = jnp.where(core == 0, low, high)
        wsend_v[step] = jnp.where(core == 0, high, low).astype(BF16)
        core_copy(step).start()

    def core_copy(step):
        return pltpu.make_async_remote_copy(
            wsend_v.at[step], wrecv_v.at[step], csend_sem.at[step], crecv_sem.at[step],
            device_id={"leaf": sibling}, device_id_type=MESH,
        )

    def spread(step):
        core_copy(step).wait_recv()
        both = (wown_v[step] + wrecv_v[step].astype(F32)).astype(BF16)
        dsend_v[step] = both.reshape(nd, rows_dp, half)
        drecv_v[step, mine] = dsend_v[step, mine]

        @pl.loop(1, nd)
        def _(i):
            to = lax.rem(mine + i, nd)
            pltpu.make_async_remote_copy(
                dsend_v.at[step, to], drecv_v.at[step, mine], dsend_sem.at[step],
                drecv_sem.at[step], device_id={"dp": to}, device_id_type=MESH,
            ).start()

    @pl.loop(0, 3)
    def _(k):
        left = jnp.concatenate([a1_v[3 * j + k] for j in range(3)], axis=0)
        leave(3 + k, dot(left, u1_v[...].reshape(3 * clips, chan), TN))

    @pl.loop(0, 3)
    def _(k):
        taps = w_v[1, pl.ds(pl.multiple_of(k * chan, chan), chan), :]
        for j in range(3):
            u0_v[3 * j + k] = (dot(u1_v[j], taps, NT) * sl0_v[3 * j + k]).astype(BF16)

    @pl.loop(0, 3)
    def _(k):
        spread(3 + k)

    @pl.loop(0, 3)
    def _(k):
        left = a_v[:, k].reshape(9 * clips, chan)
        leave(k, dot(left, u0_v[...].reshape(9 * clips, chan), TN))

    @pl.loop(0, 3)
    def _(k):
        spread(k)

    bytes_wait(hrecv_v.at[pl.ds(0, nd - 1)], h_sem.at[1])

    @pl.loop(0, span // 16)
    def _(i):
        part = pl.ds(pl.multiple_of(i * 16, 16), 16)
        total = hrecv_v[0, part, :].astype(F32)
        for d in range(1, nd):
            total = total + hrecv_v[d, part, :].astype(F32)
        head_ref[part, :] = total.astype(BF16)

    filled = 6 * rows_dp
    if g_v.shape[0] > filled:
        g_v[filled:, :] = jnp.zeros((g_v.shape[0] - filled, half), F32)

    def gather_step(step):
        bytes_wait(drecv_v.at[step, pl.ds(0, nd - 1)], drecv_sem.at[step])
        total = drecv_v[step, 0].astype(F32)
        for d in range(1, nd):
            total = total + drecv_v[step, d].astype(F32)
        g_v[pl.ds(pl.multiple_of(step * rows_dp, rows_dp), rows_dp), :] = total

    @pl.loop(0, 3)
    def _(k):
        gather_step(3 + k)

    @pl.loop(0, 3)
    def _(k):
        gather_step(k)

    zsend_v[...] = g_v[...].T.astype(BF16).reshape(nl // 2, cols_leaf, g_v.shape[0])
    my_z = me // 2
    for i in range(nl // 2):
        to = core * (nl // 2) + i

        @pl.when(to == me)
        def _():
            zrecv_v[my_z] = zsend_v[i]

        @pl.when(to != me)
        def _():
            pltpu.make_async_remote_copy(
                zsend_v.at[i], zrecv_v.at[my_z], zsend_sem.at[i], zrecv_sem.at[my_z],
                device_id={"leaf": to}, device_id_type=MESH,
            ).start()

    giver = me // (nl // 2)
    zsum_v[...] = jnp.zeros(zsum_v.shape, F32)
    for z in range(nl // 2):

        @pl.when(2 * z + giver != me)
        def _():
            pltpu.make_async_remote_copy(
                zsend_v.at[z], zrecv_v.at[z], zsend_sem.at[z], zrecv_sem.at[z],
                device_id={"leaf": sibling}, device_id_type=MESH,
            ).wait_recv()

    total = zrecv_v[0].astype(F32)
    for z in range(1, nl // 2):
        total = total + zrecv_v[z].astype(F32)
    zsum_v[0:cols_leaf, :] = total
    final = zsum_v[...].T[:filled, :cols_leaf]
    conv_ref[...] = final.reshape(2, 3, rows_dp, cols_leaf).astype(BF16)

    bytes_wait(esend_v.at[pl.ds(0, (nl - 1) * cap)], e_sem.at[0])
    bytes_wait(gsend_v.at[pl.ds(0, (nl - 1) * cap)], g_sem.at[0])
    bytes_wait(hsend_v.at[pl.ds(0, nd - 1)], h_sem.at[0])

    @pl.loop(0, 6)
    def _(step):
        core_copy(step).wait_send()
        bytes_wait(dsend_v.at[step, pl.ds(0, nd - 1)], dsend_sem.at[step])

    for i in range(nl // 2):

        @pl.when(core * (nl // 2) + i != me)
        def _():
            pltpu.make_async_remote_copy(
                zsend_v.at[i], zrecv_v.at[my_z], zsend_sem.at[i], zrecv_sem.at[my_z],
                device_id={"leaf": sibling}, device_id_type=MESH,
            ).wait_send()


def body(audio, weight, head_weight, clip_owner, node_ids, *, nd, nl):
    clips, length, chan = audio.shape
    nodes = head_weight.shape[0]
    routes = clip_owner.shape[1]
    pairs = node_ids.shape[2]
    cap = 2 * clips * routes // nl
    slots = nl * cap
    half = chan // 2
    rows_dp, cols_leaf = chan // nd, chan // nl
    filled = -(-6 * rows_dp // 128) * 128
    chunk = 48
    groups = 4 if nl >= 8 else 2
    steps = clips // chunk
    a = jnp.transpose(audio, (1, 0, 2)).reshape(length // 3, 3, clips, chan)
    w = weight.reshape(2, 3 * chan, chan)
    own = jnp.transpose(clip_owner, (1, 0))
    ids = jnp.transpose(node_ids, (1, 2, 0))
    vm = pltpu.VMEM
    dma = pltpu.SemaphoreType.DMA
    scratch = [
        vm((9, 3, clips, chan), BF16),
        vm((2, 3 * chan, chan), BF16),
        vm((nodes, chan), BF16),
        vm((chan, nodes), BF16),
        vm((9, chunk, chan), F32),
        vm((9, clips, chan), BF16),
        vm((9, clips, chan), F32),
        vm((3, clips, chan), F32),
        vm((clips, chan), BF16),
        vm((slots, clips), BF16),
        vm((slots, 128), F32),
        vm((slots, 128), F32),
        vm((slots, chan), BF16),
        vm((slots, chan), BF16),
        vm((slots, nodes), BF16),
        vm((slots, nodes), BF16),
        vm((slots, nodes), BF16),
        vm((slots, chan), BF16),
        vm((slots, chan), BF16),
        vm((nd, nodes // nd, chan), BF16),
        vm((nd, nodes // nd, chan), BF16),
        vm((3, clips, chan), BF16),
        vm((9, clips, chan), BF16),
        vm((6, chan, half), F32),
        vm((6, chan, half), BF16),
        vm((6, chan, half), BF16),
        vm((6, nd, rows_dp, half), BF16),
        vm((6, nd, rows_dp, half), BF16),
        vm((filled, half), F32),
        vm((nl // 2, cols_leaf, filled), BF16),
        vm((nl // 2, cols_leaf, filled), BF16),
        vm((max(128, cols_leaf), filled), F32),
        dma((3,)), dma((steps,)), dma((2,)), dma((1,)), dma((nl,)), dma((2,)), dma((2,)),
        dma((6,)), dma((6,)), dma((6,)), dma((6,)), dma((nl // 2,)), dma((nl // 2,)),
    ]
    whole = pl.BlockSpec(memory_space=pltpu.VMEM)
    far = pl.BlockSpec(memory_space=pl.ANY)
    return pl.pallas_call(
        functools.partial(kernel, nd, nl, chunk, groups),
        out_shape=(
            jax.ShapeDtypeStruct((2, 3, rows_dp, cols_leaf), BF16),
            jax.ShapeDtypeStruct((nodes // nd, chan), BF16),
        ),
        in_specs=[far, far, far, whole, whole],
        out_specs=(whole, whole),
        scratch_shapes=scratch,
        compiler_params=pltpu.CompilerParams(
            collective_id=0, has_side_effects=True, vmem_limit_bytes=62914560
        ),
    )(a, w, head_weight, own, ids)


def solution(mesh):
    placed = (
        P(("dp", "leaf"), None, None),
        P(),
        P("leaf", None),
        P(("dp", "leaf"), None),
        P(("dp", "leaf"), None, None),
    )
    return jax.shard_map(
        functools.partial(body, nd=mesh.shape["dp"], nl=mesh.shape["leaf"]),
        mesh=mesh,
        in_specs=placed,
        out_specs=(P(None, None, "dp", "leaf"), P(("leaf", "dp"), None)),
        check_vma=False,
    )
```

time: 413 us -> 105 us (0.25)
  waiting for transfers between devices: 186 us -> 0 us
  Pallas kernels: 0 us -> 101 us
  local copies, waits for them, and re-layouts: 91.5 us -> 2.99 us
  other arithmetic: 55.8 us -> 0 us
  matrix products: 37.6 us -> 0 us
  starting transfers between devices: 25 us -> 0 us
  between operations: 14 us -> 0.64 us
    reduce_scatter x2 -> x0, waiting for transfers between devices: 115 us -> none  [the longest x1 79 us: body(): lax.psum_scatter(head_local, 'dp', scatter_dimension=0, tiled=True)]
    pallas_call x0 -> x1, Pallas kernels: none -> 101 us  [body(): pl.pallas_call(functools.partial(kernel, nd, nl, chunk, groups), out_shap...]
    unnamed x4 -> x0, waiting for transfers between devices: 55.8 us -> none
    scatter-add x1 -> x0, other arithmetic: 45.2 us -> none  [score_routes(): jax.ops.segment_sum(terms.reshape(-1, slot_emb.shape[1]), slot_nodes.resh...]
    dot_general x7 -> x0, matrix products: 37.6 us -> none  [the longest x2 11.2 us: body(): lax.dot_general(layer_inputs[layer_index], upstream, (((0,), (0,)), ((),...]
    gather x2 -> x0, local copies, waits for them, and re-layouts: 27.5 us -> none  [the longest x1 25.4 us: score_routes(): rows_bf = head_weight[slot_nodes]]
    all_to_all x3 -> x0, starting transfers between devices: 24.4 us -> none  [the longest x1 9.98 us: body(): lax.all_to_all(send_nodes.reshape(owner_count, capacity, pair_count), 'le...]
    unnamed x19 -> x2, local copies, waits for them, and re-layouts: 19.7 us -> 2.99 us
  transfers between devices with their start and end apart: 6 -> 0, of which waited for: 4 -> 0; matrix products, arithmetic and copies ran while one was open for 31% -> 0% of each run, Pallas kernels for 0% -> 0%
where the time goes in v1:
time: 105 us; the launch traced here: 104 us
  Pallas kernels  101 us (96%)
  local copies, waits for them, and re-layouts  2.99 us (3%)
    pallas_call x1, Pallas kernels, body(): pl.pallas_call(functools.partial(kernel, nd, nl, chunk, groups), out_shap...  101 us
    unnamed x2, local copies, waits for them, and re-layouts  2.99 us

profile of v1, /device:TPU:1, one launch (start us, length us, event | category | flops | bytes accessed | tf_op | source)
XLA Modules:
  0.0 104.3 jit_solution(170556927502852176)
XLA Ops:
  0.6 100.7 %shard_map.68 = (bf16[2,3,32,32]{3,2,1,0:T(8,128)(2,1)}, bf16[128,512]{1,0:T(8,128)(2,1)}) custom-call(bf16[9,3,192,512]{3,2,1,0:T(8,128)(2,1)} %bitcast.6, bf16[2,1536,512]{2,1,0:T(8,128)(2,1)} %bitcast.7, bf16[2048,512]{1,0:T(8,128)(2,1)} %h_hbm.1, s32[2,192]{1,0:T(2,128)} %bitcast.9, s32[2,8,192]{2,1,0:T(8,128)} %bitcast.8), custom_call_target="tpu_custom_call" | custom-call | tf_op jit(solution)/shard_map/pallas_call | solution.py:454
  101.3 1.4 %copy.9 = bf16[2,3,32,32]{3,2,1,0:T(8,128)(2,1)} copy(bf16[2,3,32,32]{3,2,1,0:T(8,128)(2,1)} %get-tuple-element.4) | data formatting | bytes 24576
  102.7 1.6 %copy.10 = bf16[128,512]{1,0:T(8,128)(2,1)} copy(bf16[128,512]{1,0:T(8,128)(2,1)} %get-tuple-element.5) | data formatting | bytes 262144

commit v2 on v1

--- a/solution.py
+++ b/solution.py
@@ -1,4 +1,5 @@
 import functools
+import math
 
 import jax
 import jax.numpy as jnp
@@ -32,15 +33,16 @@
 
 
 def kernel(
-    nd, nl, chunk, groups,
+    ny, nx, nl, chunk, groups,
     a_hbm, w_hbm, h_hbm, own_ref, node_ref,
     conv_ref, head_ref,
-    a_v, w_v, h_v, ht_v, p_v, a1_v, sl0_v, sl1_v, emb_v, d_v,
+    a_v, w_v, h_v, ht_v, pa_v, pb_v, a1_v, sl0_v, sl1_v, emb_v, d_v,
     nsend_v, nrecv_v, esend_v, erecv_v, call_v, cpos_v, st_v, gsend_v, grecv_v,
-    hsend_v, hrecv_v, u1_v, u0_v, wown_v, wsend_v, wrecv_v, dsend_v, drecv_v,
+    hsend_v, hone_v, hmid_v, htwo_v, u1_v, u0_v, wown_v, wsend_v, wrecv_v,
+    dsend_v, done_v, dmid_v, dtwo_v,
     g_v, zsend_v, zrecv_v, zsum_v,
     load_sem, a_sem, n_sem, e_sem, erecv_sem, g_sem, h_sem, csend_sem, crecv_sem,
-    dsend_sem, drecv_sem, zsend_sem, zrecv_sem,
+    d_sem, zsend_sem, zrecv_sem,
 ):
     me = lax.axis_index("leaf")
     mine = lax.axis_index("dp")
@@ -52,6 +54,8 @@
     slots = nl * cap
     nodes = h_v.shape[0]
     pairs = node_ref.shape[1]
+    nd = ny * nx
+    my_y, my_x = mine // nx, lax.rem(mine, nx)
     half = chan // 2
     span = nodes // nd
     rows_dp = chan // nd
@@ -92,27 +96,29 @@
         < lax.broadcasted_iota(jnp.int32, (clips, clips), 1)
     ).astype(F32).astype(BF16)
     slot_iota = lax.broadcasted_iota(jnp.int32, (slots, clips), 0)
+    list_iota = lax.broadcasted_iota(jnp.int32, (nl * 128, clips), 0)
     base = jnp.zeros((nl, 1), F32)
     spots = []
-    lists = jnp.zeros((slots, 128), F32)
+    lists = jnp.zeros((2 * pairs, nl * 128), F32)
     for r in range(2):
         hit = (own_ref[r : r + 1, :] == owner_iota).astype(F32)
         rank = dot(hit.astype(BF16), before) + base
         base = base + jnp.sum(hit, axis=1, keepdims=True)
-        place = jnp.sum(hit * (rank + (owner_iota * cap).astype(F32)), axis=0, keepdims=True)
-        spot = (slot_iota == place.astype(jnp.int32)).astype(F32).astype(BF16)
-        spots.append(spot)
+
+        def place(stride):
+            spot = jnp.sum(
+                hit * (rank + (owner_iota * stride).astype(F32)), axis=0, keepdims=True
+            )
+            return spot.astype(jnp.int32)
+
+        spots.append((slot_iota == place(cap)).astype(F32).astype(BF16))
+        wide = (list_iota == place(128)).astype(F32).astype(BF16)
         ident = node_ref[r] + 1
-        upper = (ident >> 7).astype(F32)
-        lower = (ident & 127).astype(F32)
-        pad = jnp.zeros((128 - pairs, clips), F32)
-        upper = jnp.concatenate([upper, pad], axis=0).astype(BF16)
-        lower = jnp.concatenate([lower, pad], axis=0).astype(BF16)
-        lists = lists + dot(spot, upper, NT) * 128.0 + dot(spot, lower, NT)
+        parts = jnp.concatenate([ident >> 7, ident & 127], axis=0).astype(F32).astype(BF16)
+        lists = lists + dot(parts, wide, NT)
     d_v[...] = spots[0] + spots[1]
-    nsend_v[...] = lists - 1.0
-
-    pl.semaphore_wait(barrier, nl - 1 + nd - 1)
+    for o in range(nl):
+        nsend_v[o] = lists[:, o * 128 : (o + 1) * 128].astype(BF16)
 
     def block(i):
         return pl.ds(pl.multiple_of(i * cap, cap), cap)
@@ -126,32 +132,32 @@
             return [group * per + lax.rem(inside + o, per) for o in range(1, per)]
         return [lax.rem(group + t, groups) * per + o for o in range(per)]
 
-    nrecv_v[block(me), :] = nsend_v[block(me), :]
-
-    @pl.loop(1, nl)
-    def _(i):
-        to = lax.rem(me + i, nl)
-        pltpu.make_async_remote_copy(
-            nsend_v.at[block(to)], nrecv_v.at[block(me)], n_sem.at[0], n_sem.at[1],
-            device_id={"leaf": to}, device_id_type=MESH,
-        ).start()
-
     load_w0.wait()
 
-    @pl.loop(0, steps)
-    def _(i):
+    stage = [pa_v, pb_v]
+
+    def multiply(i):
         load_a(i).wait()
-        part = pl.ds(pl.multiple_of(i * chunk, chunk), chunk)
+        part = pl.ds(i * chunk, chunk)
         folded = jnp.concatenate(
             [a_v[:, k, part, :].reshape(9 * chunk, chan) for k in range(3)], axis=1
         )
-        p_v[...] = dot(folded, w_v[0]).reshape(9, chunk, chan)
-
-        @pl.loop(0, 9)
+        stage[i % 2][...] = dot(folded, w_v[0]).reshape(9, chunk, chan)
+
+    def activate(i):
+        part = pl.ds(i * chunk, chunk)
+
+        @pl.loop(0, 9, unroll=True)
         def _(j):
-            act, slope = gelu_pair(p_v[j])
+            act, slope = gelu_pair(stage[i % 2][j])
             a1_v[j, part, :] = act.astype(BF16)
             sl0_v[j, part, :] = slope
+
+    multiply(0)
+    for i in range(steps):
+        if i + 1 < steps:
+            multiply(i + 1)
+        activate(i)
 
     load_w1.wait()
 
@@ -170,6 +176,17 @@
             total = total + act
         emb_v[part, :] = (total * (1.0 / 3.0)).astype(BF16)
 
+    pl.semaphore_wait(barrier, nl - 1 + nd - 1)
+    nrecv_v[me] = nsend_v[me]
+
+    @pl.loop(1, nl)
+    def _(i):
+        to = lax.rem(me + i, nl)
+        pltpu.make_async_remote_copy(
+            nsend_v.at[to], nrecv_v.at[me], n_sem.at[0], n_sem.at[1],
+            device_id={"leaf": to}, device_id_type=MESH,
+        ).start()
+
     esend_v[...] = dot(d_v[...], emb_v[...]).astype(BF16)
     erecv_v[block(me), :] = esend_v[block(me), :]
 
@@ -189,21 +206,24 @@
     for i in range(4):
         ht_v[:, i * piece : (i + 1) * piece] = h_v[i * piece : (i + 1) * piece, :].T
 
-    bytes_wait(nsend_v.at[pl.ds(0, (nl - 1) * cap)], n_sem.at[0])
-    bytes_wait(nrecv_v.at[pl.ds(0, (nl - 1) * cap)], n_sem.at[1])
+    bytes_wait(nsend_v.at[pl.ds(0, nl - 1)], n_sem.at[0])
+    bytes_wait(nrecv_v.at[pl.ds(0, nl - 1)], n_sem.at[1])
     node_iota = lax.broadcasted_iota(jnp.int32, (16, nodes), 1).astype(F32)
 
-    @pl.loop(0, slots // 16)
-    def _(i):
-        part = pl.ds(pl.multiple_of(i * 16, 16), 16)
-        named = nrecv_v[part, :]
-        tally = jnp.zeros((16, nodes), F32)
-        for q in range(pairs):
-            weight = 17.0 if q < pairs // 2 else 1.0
-            tally = tally + jnp.where(named[:, q : q + 1] == node_iota, weight, 0.0)
-        positive = jnp.floor(tally * (1.0 / 16.0))
-        cpos_v[part, :] = positive.astype(BF16)
-        call_v[part, :] = (tally - 16.0 * positive).astype(BF16)
+    @pl.loop(0, nl)
+    def _(o):
+        parts = nrecv_v[o].astype(F32)
+        named = (parts[:pairs] * 128.0 + parts[pairs:] - 1.0).T
+        for i in range(cap // 16):
+            part = pl.ds(pl.multiple_of(o * cap + i * 16, 16), 16)
+            tally = jnp.zeros((16, nodes), F32)
+            for q in range(pairs):
+                weight = 17.0 if q < pairs // 2 else 1.0
+                ident = named[i * 16 : (i + 1) * 16, q : q + 1]
+                tally = tally + jnp.where(ident == node_iota, weight, 0.0)
+            positive = jnp.floor(tally * (1.0 / 16.0))
+            cpos_v[part, :] = positive.astype(BF16)
+            call_v[part, :] = (tally - 16.0 * positive).astype(BF16)
 
     lanes = nodes // 4
     for t in range(groups):
@@ -242,20 +262,50 @@
                 device_id={"leaf": to}, device_id_type=MESH,
             ).start()
 
-    @pl.loop(0, nd)
+    low_rows, high_rows = pl.ds(0, span // 2), pl.ds(span // 2, span // 2)
+
+    def over_x(o):
+        return {"dp": my_y * nx + lax.rem(my_x + o, nx)}
+
+    def over_y(o):
+        return {"dp": lax.rem(my_y + o, ny) * nx + my_x}
+
+    def send(source, target, sems, device):
+        pltpu.make_async_remote_copy(
+            source, target, sems.at[0], sems.at[1], device_id=device, device_id_type=MESH
+        ).start()
+
+    for o in range(1, ny + 1):
+        y = lax.rem(my_y + o, ny)
+        cols = pl.ds(pl.multiple_of(y * nx * span, nx * span), nx * span)
+        terms = dot(st_v[:, cols], erecv_v[...], TN).astype(BF16)
+        hsend_v[y] = terms.reshape(nx, span, chan)
+        if o < ny:
+            send(hsend_v.at[y, :, high_rows], hone_v.at[1, o - 1], h_sem.at[1], over_y(o))
+    for o in range(1, nx):
+        x = lax.rem(my_x + o, nx)
+        send(hsend_v.at[:, x, low_rows], hone_v.at[0, o - 1], h_sem.at[0], over_x(o))
+
+    bytes_wait(hone_v.at[1], h_sem.at[1, 1])
+    bytes_wait(hone_v.at[0], h_sem.at[0, 1])
+    strip = 32
+
+    @pl.loop(0, ny)
     def _(i):
-        to = lax.rem(mine + i, nd)
-        cols = pl.ds(pl.multiple_of(to * span, span), span)
-        hsend_v[to] = dot(st_v[:, cols], erecv_v[...], TN).astype(BF16)
-
-        @pl.when(i > 0)
-        def _():
-            pltpu.make_async_remote_copy(
-                hsend_v.at[to], hrecv_v.at[mine], h_sem.at[0], h_sem.at[1],
-                device_id={"dp": to}, device_id_type=MESH,
-            ).start()
-
-    hrecv_v[mine] = hsend_v[mine]
+        for at in range(0, span // 2, strip):
+            part = pl.ds(at, strip)
+            total = hsend_v[i, my_x, part, :].astype(F32)
+            for o in range(nx - 1):
+                total = total + hone_v[0, o, i, part, :].astype(F32)
+            hmid_v[0, i, part, :] = total.astype(BF16)
+            total = hsend_v[my_y, i, pl.ds(span // 2 + at, strip), :].astype(F32)
+            for o in range(ny - 1):
+                total = total + hone_v[1, o, i, part, :].astype(F32)
+            hmid_v[1, i, part, :] = total.astype(BF16)
+
+    for o in range(1, ny):
+        send(hmid_v.at[0, lax.rem(my_y + o, ny)], htwo_v.at[0, o - 1], h_sem.at[2], over_y(o))
+        send(hmid_v.at[1, lax.rem(my_x + o, nx)], htwo_v.at[1, o - 1], h_sem.at[3], over_x(o))
 
     bytes_wait(grecv_v.at[pl.ds(0, (nl - 1) * cap)], g_sem.at[1])
     clip_grad = dot(d_v[...], grecv_v[...], TN) * (1.0 / 3.0)
@@ -274,19 +324,55 @@
             device_id={"leaf": sibling}, device_id_type=MESH,
         )
 
+    part_rows = rows_dp // 2
+    low_part, high_part = pl.ds(0, part_rows), pl.ds(part_rows, part_rows)
+
     def spread(step):
         core_copy(step).wait_recv()
         both = (wown_v[step] + wrecv_v[step].astype(F32)).astype(BF16)
-        dsend_v[step] = both.reshape(nd, rows_dp, half)
-        drecv_v[step, mine] = dsend_v[step, mine]
-
-        @pl.loop(1, nd)
-        def _(i):
-            to = lax.rem(mine + i, nd)
-            pltpu.make_async_remote_copy(
-                dsend_v.at[step, to], drecv_v.at[step, mine], dsend_sem.at[step],
-                drecv_sem.at[step], device_id={"dp": to}, device_id_type=MESH,
-            ).start()
+        dsend_v[step] = both.reshape(ny, nx, rows_dp, half)
+        for o in range(1, nx):
+            x = lax.rem(my_x + o, nx)
+            send(
+                dsend_v.at[step, :, x, low_part], done_v.at[step, 0, o - 1],
+                d_sem.at[step, 0], over_x(o),
+            )
+        for o in range(1, ny):
+            y = lax.rem(my_y + o, ny)
+            send(
+                dsend_v.at[step, y, :, high_part], done_v.at[step, 1, o - 1],
+                d_sem.at[step, 1], over_y(o),
+            )
+
+    def respread(step):
+        bytes_wait(done_v.at[step, 0], d_sem.at[step, 0, 1])
+        total = dsend_v[step, :, my_x, low_part, :].astype(F32)
+        for o in range(nx - 1):
+            total = total + done_v[step, 0, o].astype(F32)
+        dmid_v[step, 0] = total.astype(BF16)
+        bytes_wait(done_v.at[step, 1], d_sem.at[step, 1, 1])
+        total = dsend_v[step, my_y, :, high_part, :].astype(F32)
+        for o in range(ny - 1):
+            total = total + done_v[step, 1, o].astype(F32)
+        dmid_v[step, 1] = total.astype(BF16)
+        for o in range(1, ny):
+            send(
+                dmid_v.at[step, 0, lax.rem(my_y + o, ny)], dtwo_v.at[step, 0, o - 1],
+                d_sem.at[step, 2], over_y(o),
+            )
+            send(
+                dmid_v.at[step, 1, lax.rem(my_x + o, nx)], dtwo_v.at[step, 1, o - 1],
+                d_sem.at[step, 3], over_x(o),
+            )
+
+    def gather_step(step):
+        for side, place in ((0, my_y), (1, my_x)):
+            bytes_wait(dtwo_v.at[step, side], d_sem.at[step, 2 + side, 1])
+            total = dmid_v[step, side, place].astype(F32)
+            for o in range(ny - 1):
+                total = total + dtwo_v[step, side, o].astype(F32)
+            first = pl.multiple_of(step * rows_dp + side * part_rows, part_rows)
+            g_v[pl.ds(first, part_rows), :] = total
 
     @pl.loop(0, 3)
     def _(k):
@@ -308,30 +394,32 @@
         left = a_v[:, k].reshape(9 * clips, chan)
         leave(k, dot(left, u0_v[...].reshape(9 * clips, chan), TN))
 
-    @pl.loop(0, 3)
-    def _(k):
-        spread(k)
-
-    bytes_wait(hrecv_v.at[pl.ds(0, nd - 1)], h_sem.at[1])
-
-    @pl.loop(0, span // 16)
-    def _(i):
-        part = pl.ds(pl.multiple_of(i * 16, 16), 16)
-        total = hrecv_v[0, part, :].astype(F32)
-        for d in range(1, nd):
-            total = total + hrecv_v[d, part, :].astype(F32)
-        head_ref[part, :] = total.astype(BF16)
+        @pl.when(k > 0)
+        def _():
+            spread(k - 1)
+
+    spread(2)
 
     filled = 6 * rows_dp
     if g_v.shape[0] > filled:
         g_v[filled:, :] = jnp.zeros((g_v.shape[0] - filled, half), F32)
 
-    def gather_step(step):
-        bytes_wait(drecv_v.at[step, pl.ds(0, nd - 1)], drecv_sem.at[step])
-        total = drecv_v[step, 0].astype(F32)
-        for d in range(1, nd):
-            total = total + drecv_v[step, d].astype(F32)
-        g_v[pl.ds(pl.multiple_of(step * rows_dp, rows_dp), rows_dp), :] = total
+    @pl.loop(0, 3)
+    def _(k):
+        respread(3 + k)
+
+    @pl.loop(0, 3)
+    def _(k):
+        respread(k)
+
+    for side, place in ((0, my_y), (1, my_x)):
+        bytes_wait(htwo_v.at[side], h_sem.at[2 + side, 1])
+        for at in range(0, span // 2, strip):
+            part = pl.ds(at, strip)
+            total = hmid_v[side, place, part, :].astype(F32)
+            for o in range(ny - 1):
+                total = total + htwo_v[side, o, part, :].astype(F32)
+            head_ref[pl.ds(side * (span // 2) + at, strip), :] = total.astype(BF16)
 
     @pl.loop(0, 3)
     def _(k):
@@ -377,12 +465,16 @@
 
     bytes_wait(esend_v.at[pl.ds(0, (nl - 1) * cap)], e_sem.at[0])
     bytes_wait(gsend_v.at[pl.ds(0, (nl - 1) * cap)], g_sem.at[0])
-    bytes_wait(hsend_v.at[pl.ds(0, nd - 1)], h_sem.at[0])
+    for side in range(2):
+        bytes_wait(hone_v.at[side], h_sem.at[side, 0])
+        bytes_wait(htwo_v.at[side], h_sem.at[2 + side, 0])
 
     @pl.loop(0, 6)
     def _(step):
         core_copy(step).wait_send()
-        bytes_wait(dsend_v.at[step, pl.ds(0, nd - 1)], dsend_sem.at[step])
+        for side in range(2):
+            bytes_wait(done_v.at[step, side], d_sem.at[step, side, 0])
+            bytes_wait(dtwo_v.at[step, side], d_sem.at[step, 2 + side, 0])
 
     for i in range(nl // 2):
 
@@ -395,6 +487,8 @@
 
 
 def body(audio, weight, head_weight, clip_owner, node_ids, *, nd, nl):
+    nx = math.isqrt(nd)
+    ny = nd // nx
     clips, length, chan = audio.shape
     nodes = head_weight.shape[0]
     routes = clip_owner.shape[1]
@@ -403,6 +497,7 @@
     slots = nl * cap
     half = chan // 2
     rows_dp, cols_leaf = chan // nd, chan // nl
+    span = nodes // nd
     filled = -(-6 * rows_dp // 128) * 128
     chunk = 48
     groups = 4 if nl >= 8 else 2
@@ -419,13 +514,14 @@
         vm((nodes, chan), BF16),
         vm((chan, nodes), BF16),
         vm((9, chunk, chan), F32),
+        vm((9, chunk, chan), F32),
         vm((9, clips, chan), BF16),
         vm((9, clips, chan), F32),
         vm((3, clips, chan), F32),
         vm((clips, chan), BF16),
         vm((slots, clips), BF16),
-        vm((slots, 128), F32),
-        vm((slots, 128), F32),
+        vm((nl, 2 * pairs, 128), BF16),
+        vm((nl, 2 * pairs, 128), BF16),
         vm((slots, chan), BF16),
         vm((slots, chan), BF16),
         vm((slots, nodes), BF16),
@@ -433,26 +529,30 @@
         vm((slots, nodes), BF16),
         vm((slots, chan), BF16),
         vm((slots, chan), BF16),
-        vm((nd, nodes // nd, chan), BF16),
-        vm((nd, nodes // nd, chan), BF16),
+        vm((ny, nx, span, chan), BF16),
+        vm((2, ny - 1, ny, span // 2, chan), BF16),
+        vm((2, ny, span // 2, chan), BF16),
+        vm((2, ny - 1, span // 2, chan), BF16),
         vm((3, clips, chan), BF16),
         vm((9, clips, chan), BF16),
         vm((6, chan, half), F32),
         vm((6, chan, half), BF16),
         vm((6, chan, half), BF16),
-        vm((6, nd, rows_dp, half), BF16),
-        vm((6, nd, rows_dp, half), BF16),
+        vm((6, ny, nx, rows_dp, half), BF16),
+        vm((6, 2, ny - 1, ny, rows_dp // 2, half), BF16),
+        vm((6, 2, ny, rows_dp // 2, half), BF16),
+        vm((6, 2, ny - 1, rows_dp // 2, half), BF16),
         vm((filled, half), F32),
         vm((nl // 2, cols_leaf, filled), BF16),
         vm((nl // 2, cols_leaf, filled), BF16),
         vm((max(128, cols_leaf), filled), F32),
-        dma((3,)), dma((steps,)), dma((2,)), dma((1,)), dma((nl,)), dma((2,)), dma((2,)),
-        dma((6,)), dma((6,)), dma((6,)), dma((6,)), dma((nl // 2,)), dma((nl // 2,)),
+        dma((3,)), dma((steps,)), dma((2,)), dma((1,)), dma((nl,)), dma((2,)), dma((4, 2)),
+        dma((6,)), dma((6,)), dma((6, 4, 2)), dma((nl // 2,)), dma((nl // 2,)),
     ]
     whole = pl.BlockSpec(memory_space=pltpu.VMEM)
     far = pl.BlockSpec(memory_space=pl.ANY)
     return pl.pallas_call(
-        functools.partial(kernel, nd, nl, chunk, groups),
+        functools.partial(kernel, ny, nx, nl, chunk, groups),
         out_shape=(
             jax.ShapeDtypeStruct((2, 3, rows_dp, cols_leaf), BF16),
             jax.ShapeDtypeStruct((nodes // nd, chan), BF16),

time: 105 us -> 88 us (0.84)
  Pallas kernels: 101 us -> 84.1 us
    pallas_call x1, Pallas kernels: 101 us -> 84.1 us  [body(): pl.pallas_call(functools.partial(kernel, ny, nx, nl, chunk, groups), out_...]
where the time goes in v2:
time: 88 us; the launch traced here: 87.8 us
  Pallas kernels  84.1 us (96%)
  local copies, waits for them, and re-layouts  2.99 us (3%)
    pallas_call x1, Pallas kernels, body(): pl.pallas_call(functools.partial(kernel, ny, nx, nl, chunk, groups), out_...  84.1 us
    unnamed x2, local copies, waits for them, and re-layouts  2.99 us

profile of v2, /device:TPU:1, one launch (start us, length us, event | category | flops | bytes accessed | tf_op | source)
XLA Modules:
  0.0 87.8 jit_solution(6044923439045766098)
XLA Ops:
  0.6 84.1 %shard_map.68 = (bf16[2,3,32,32]{3,2,1,0:T(8,128)(2,1)}, bf16[128,512]{1,0:T(8,128)(2,1)}) custom-call(bf16[9,3,192,512]{3,2,1,0:T(8,128)(2,1)} %bitcast.6, bf16[2,1536,512]{2,1,0:T(8,128)(2,1)} %bitcast.7, bf16[2048,512]{1,0:T(8,128)(2,1)} %h_hbm.1, s32[2,192]{1,0:T(2,128)} %bitcast.9, s32[2,8,192]{2,1,0:T(8,128)} %bitcast.8), custom_call_target="tpu_custom_call" | custom-call | tf_op jit(solution)/shard_map/pallas_call | solution.py:554
  84.8 1.4 %copy.9 = bf16[2,3,32,32]{3,2,1,0:T(8,128)(2,1)} copy(bf16[2,3,32,32]{3,2,1,0:T(8,128)(2,1)} %get-tuple-element.4) | data formatting | bytes 24576
  86.2 1.6 %copy.10 = bf16[128,512]{1,0:T(8,128)(2,1)} copy(bf16[128,512]{1,0:T(8,128)(2,1)} %get-tuple-element.5) | data formatting | bytes 262144

commit v3 on v2

--- a/solution.py
+++ b/solution.py
@@ -33,7 +33,7 @@
 
 
 def kernel(
-    ny, nx, nl, chunk, groups,
+    ny, nx, nl, chunk,
     a_hbm, w_hbm, h_hbm, own_ref, node_ref,
     conv_ref, head_ref,
     a_v, w_v, h_v, ht_v, pa_v, pb_v, a1_v, sl0_v, sl1_v, emb_v, d_v,
@@ -123,14 +123,27 @@
     def block(i):
         return pl.ds(pl.multiple_of(i * cap, cap), cap)
 
-    per = nl // groups
-    group = me // per
-    inside = lax.rem(me, per)
-
-    def peers(t):
-        if t == 0:
-            return [group * per + lax.rem(inside + o, per) for o in range(1, per)]
-        return [lax.rem(group + t, groups) * per + o for o in range(per)]
+    nz = nl // 2
+    my_z = me // 2
+    order = []
+    for d in range(nz // 2 - 1, 0, -1):
+        order.append((d, nz - d))
+    order.insert(min(1, len(order)), (nz // 2, 0))
+    order = [rel for pair in order for rel in pair]
+    per = 4
+
+    def leaf_at(rel, c):
+        return 2 * lax.rem(my_z + rel, nz) + c
+
+    def turn(rel):
+        return order.index(rel % nz)
+
+    def away():
+        for rel in order:
+            for c in range(2) if rel else (1 - core,):
+                yield leaf_at(rel, c), 2 * turn(rel) + c, 2 * turn(-rel) + core
+
+    home = 2 * turn(0) + core
 
     load_w0.wait()
 
@@ -161,44 +174,37 @@
 
     load_w1.wait()
 
-    @pl.loop(0, 3)
-    def _(j):
-        folded = jnp.concatenate([a1_v[3 * j + k] for k in range(3)], axis=1)
-        sl1_v[j] = dot(folded, w_v[1])
-
-    @pl.loop(0, steps)
-    def _(i):
-        part = pl.ds(pl.multiple_of(i * chunk, chunk), chunk)
-        total = jnp.zeros((chunk, chan), F32)
+    for side in range(2):
+        cols = pl.ds(side * half, half)
         for j in range(3):
-            act, slope = gelu_pair(sl1_v[j, part, :])
-            sl1_v[j, part, :] = slope
-            total = total + act
-        emb_v[part, :] = (total * (1.0 / 3.0)).astype(BF16)
-
-    pl.semaphore_wait(barrier, nl - 1 + nd - 1)
-    nrecv_v[me] = nsend_v[me]
-
-    @pl.loop(1, nl)
-    def _(i):
-        to = lax.rem(me + i, nl)
-        pltpu.make_async_remote_copy(
-            nsend_v.at[to], nrecv_v.at[me], n_sem.at[0], n_sem.at[1],
-            device_id={"leaf": to}, device_id_type=MESH,
-        ).start()
-
-    esend_v[...] = dot(d_v[...], emb_v[...]).astype(BF16)
-    erecv_v[block(me), :] = esend_v[block(me), :]
-
-    def emb_copy(to, source):
-        return pltpu.make_async_remote_copy(
-            esend_v.at[block(to)], erecv_v.at[block(source)], e_sem.at[0],
-            erecv_sem.at[source], device_id={"leaf": to}, device_id_type=MESH,
-        )
-
-    for t in range(groups):
-        for to in peers(t):
-            emb_copy(to, me).start()
+            folded = jnp.concatenate([a1_v[3 * j + k] for k in range(3)], axis=1)
+            sl1_v[j, :, cols] = dot(folded, w_v[1, :, cols])
+
+        @pl.loop(0, steps)
+        def _(i):
+            part = pl.ds(pl.multiple_of(i * chunk, chunk), chunk)
+            total = jnp.zeros((chunk, half), F32)
+            for j in range(3):
+                act, slope = gelu_pair(sl1_v[j, part, cols])
+                sl1_v[j, part, cols] = slope
+                total = total + act
+            emb_v[part, cols] = (total * (1.0 / 3.0)).astype(BF16)
+
+        esend_v[:, cols] = dot(d_v[...], emb_v[:, cols]).astype(BF16)
+        if side == 0:
+            pl.semaphore_wait(barrier, nl - 1 + nd - 1)
+            nrecv_v[home] = nsend_v[me]
+            for to, _, mark in away():
+                pltpu.make_async_remote_copy(
+                    nsend_v.at[to], nrecv_v.at[mark], n_sem.at[0], n_sem.at[1],
+                    device_id={"leaf": to}, device_id_type=MESH,
+                ).start()
+        for to, _, mark in away():
+            pltpu.make_async_remote_copy(
+                esend_v.at[block(to), cols], erecv_v.at[block(mark), cols], e_sem.at[0],
+                erecv_sem.at[mark], device_id={"leaf": to}, device_id_type=MESH,
+            ).start()
+    erecv_v[block(home), :] = esend_v[block(me), :]
 
     load_h.wait()
     piece = nodes // 4
@@ -226,19 +232,14 @@
             call_v[part, :] = (tally - 16.0 * positive).astype(BF16)
 
     lanes = nodes // 4
-    for t in range(groups):
-        source_group = lax.rem(group + groups - t, groups)
-        for i in range(per):
-            source = source_group * per + i
-            if t == 0:
-
-                @pl.when(source != me)
-                def _():
-                    emb_copy(source, source).wait_recv()
-            else:
-                emb_copy(source, source).wait_recv()
-        start = pl.multiple_of(source_group * (per * cap), per * cap)
-        rows = pl.ds(start, per * cap)
+    for t in range(nl // per):
+        sources = []
+        for rel in order[2 * t : 2 * t + 2]:
+            for c in range(2) if rel else (1 - core,):
+                sources.append((leaf_at(rel, c), 2 * turn(rel) + c))
+        for _, place in sources:
+            bytes_wait(erecv_v.at[block(place)], erecv_sem.at[place])
+        rows = pl.ds(t * per * cap, per * cap)
         emb = erecv_v[rows, :]
 
         @pl.loop(0, 4)
@@ -251,14 +252,11 @@
             ).astype(BF16)
 
         gsend_v[rows, :] = dot(st_v[rows, :], h_v[...]).astype(BF16)
-        if t == 0:
-            grecv_v[block(me), :] = gsend_v[block(me), :]
-            back = [group * per + lax.rem(inside + o, per) for o in range(1, per)]
-        else:
-            back = [source_group * per + o for o in range(per)]
-        for to in back:
+        if 0 in order[2 * t : 2 * t + 2]:
+            grecv_v[block(me), :] = gsend_v[block(home), :]
+        for to, place in sources:
             pltpu.make_async_remote_copy(
-                gsend_v.at[block(to)], grecv_v.at[block(me)], g_sem.at[0], g_sem.at[1],
+                gsend_v.at[block(place)], grecv_v.at[block(me)], g_sem.at[0], g_sem.at[1],
                 device_id={"leaf": to}, device_id_type=MESH,
             ).start()
 
@@ -430,7 +428,6 @@
         gather_step(k)
 
     zsend_v[...] = g_v[...].T.astype(BF16).reshape(nl // 2, cols_leaf, g_v.shape[0])
-    my_z = me // 2
     for i in range(nl // 2):
         to = core * (nl // 2) + i
 
@@ -484,6 +481,11 @@
                 zsend_v.at[i], zrecv_v.at[my_z], zsend_sem.at[i], zrecv_sem.at[my_z],
                 device_id={"leaf": sibling}, device_id_type=MESH,
             ).wait_send()
+
+
+def hand_on(conv_ref, head_ref, conv_out, head_out):
+    conv_out[...] = conv_ref[...]
+    head_out[...] = head_ref[...]
 
 
 def body(audio, weight, head_weight, clip_owner, node_ids, *, nd, nl):
@@ -500,7 +502,6 @@
     span = nodes // nd
     filled = -(-6 * rows_dp // 128) * 128
     chunk = 48
-    groups = 4 if nl >= 8 else 2
     steps = clips // chunk
     a = jnp.transpose(audio, (1, 0, 2)).reshape(length // 3, 3, clips, chan)
     w = weight.reshape(2, 3 * chan, chan)
@@ -551,8 +552,8 @@
     ]
     whole = pl.BlockSpec(memory_space=pltpu.VMEM)
     far = pl.BlockSpec(memory_space=pl.ANY)
-    return pl.pallas_call(
-        functools.partial(kernel, ny, nx, nl, chunk, groups),
+    conv, head = pl.pallas_call(
+        functools.partial(kernel, ny, nx, nl, chunk),
         out_shape=(
             jax.ShapeDtypeStruct((2, 3, rows_dp, cols_leaf), BF16),
             jax.ShapeDtypeStruct((nodes // nd, chan), BF16),
@@ -564,6 +565,15 @@
             collective_id=0, has_side_effects=True, vmem_limit_bytes=62914560
         ),
     )(a, w, head_weight, own, ids)
+    return pl.pallas_call(
+        hand_on,
+        out_shape=(
+            jax.ShapeDtypeStruct(conv.shape, BF16),
+            jax.ShapeDtypeStruct(head.shape, BF16),
+        ),
+        in_specs=[whole, whole],
+        out_specs=(whole, whole),
+    )(conv, head)
 
 
 def solution(mesh):

time: 88 us -> 85.6 us (0.973)
  local copies, waits for them, and re-layouts: 2.99 us -> 0 us
    unnamed x2 -> x0, local copies, waits for them, and re-layouts: 2.99 us -> none
    pallas_call x1 -> x2, Pallas kernels: 84.1 us -> 84.8 us  [the longest x1 83.2 us: body(): pl.pallas_call(functools.partial(kernel, ny, nx, nl, chunk), out_shape=(j...]
where the time goes in v3:
time: 85.6 us; the launch traced here: 85.4 us
  Pallas kernels  84.8 us (99%)
    pallas_call x1, Pallas kernels, body(): pl.pallas_call(functools.partial(kernel, ny, nx, nl, chunk), out_shape=(j...  83.2 us

profile of v3, /device:TPU:1, one launch (start us, length us, event | category | flops | bytes accessed | tf_op | source)
XLA Modules:
  0.0 85.4 jit_solution(2811455495069233355)
XLA Ops:
  0.6 83.2 %shard_map.68 = (bf16[2,3,32,32]{3,2,1,0:T(8,128)(2,1)}, bf16[128,512]{1,0:T(8,128)(2,1)}) custom-call(bf16[9,3,192,512]{3,2,1,0:T(8,128)(2,1)} %bitcast.6, bf16[2,1536,512]{2,1,0:T(8,128)(2,1)} %bitcast.7, bf16[2048,512]{1,0:T(8,128)(2,1)} %h_hbm.1, s32[2,192]{1,0:T(2,128)} %bitcast.9, s32[2,8,192]{2,1,0:T(8,128)} %bitcast.8), custom_call_target="tpu_custom_call" | custom-call | tf_op jit(solution)/shard_map/pallas_call | solution.py:555
  83.8 1.6 %shard_map.69 = (bf16[2,3,32,32]{3,2,1,0:T(8,128)(2,1)}, bf16[128,512]{1,0:T(8,128)(2,1)}) custom-call(bf16[2,3,32,32]{3,2,1,0:T(8,128)(2,1)} %get-tuple-element.4.conv_ref, bf16[128,512]{1,0:T(8,128)(2,1)} %get-tuple-element.5.head_ref), custom_call_target="tpu_custom_call" | custom-call | tf_op jit(solution)/shard_map/pallas_call | solution.py:568

commit v4 on v3

--- a/solution.py
+++ b/solution.py
@@ -38,8 +38,8 @@
     conv_ref, head_ref,
     a_v, w_v, h_v, ht_v, pa_v, pb_v, a1_v, sl0_v, sl1_v, emb_v, d_v,
     nsend_v, nrecv_v, esend_v, erecv_v, call_v, cpos_v, st_v, gsend_v, grecv_v,
-    hsend_v, hone_v, hmid_v, htwo_v, u1_v, u0_v, wown_v, wsend_v, wrecv_v,
-    dsend_v, done_v, dmid_v, dtwo_v,
+    hsend_v, hfar_v, hnear_v, hsum_v, hgot_v, hmid_v, htwo_v, u1_v, u0_v, wown_v, wsend_v, wrecv_v,
+    dsend_v, dfar_v, dnear_v, dsum_v, dgot_v, dmid_v, dtwo_v,
     g_v, zsend_v, zrecv_v, zsum_v,
     load_sem, a_sem, n_sem, e_sem, erecv_sem, g_sem, h_sem, csend_sem, crecv_sem,
     d_sem, zsend_sem, zrecv_sem,
@@ -180,7 +180,7 @@
             folded = jnp.concatenate([a1_v[3 * j + k] for k in range(3)], axis=1)
             sl1_v[j, :, cols] = dot(folded, w_v[1, :, cols])
 
-        @pl.loop(0, steps)
+        @pl.loop(0, steps, unroll=True)
         def _(i):
             part = pl.ds(pl.multiple_of(i * chunk, chunk), chunk)
             total = jnp.zeros((chunk, half), F32)
@@ -228,8 +228,9 @@
                 ident = named[i * 16 : (i + 1) * 16, q : q + 1]
                 tally = tally + jnp.where(ident == node_iota, weight, 0.0)
             positive = jnp.floor(tally * (1.0 / 16.0))
-            cpos_v[part, :] = positive.astype(BF16)
-            call_v[part, :] = (tally - 16.0 * positive).astype(BF16)
+            every = 0.5 * tally - 8.0 * positive
+            call_v[part, :] = every.astype(BF16)
+            cpos_v[part, :] = (every - positive).astype(BF16)
 
     lanes = nodes // 4
     for t in range(nl // per):
@@ -242,13 +243,12 @@
         rows = pl.ds(t * per * cap, per * cap)
         emb = erecv_v[rows, :]
 
-        @pl.loop(0, 4)
-        def _(n):
-            cols = pl.ds(pl.multiple_of(n * lanes, lanes), lanes)
+        for n in range(4):
+            cols = pl.ds(n * lanes, lanes)
             score = dot(emb, ht_v[:, cols])
-            sig = 0.5 * jnp.tanh(0.5 * score) + 0.5
             st_v[rows, cols] = (
-                sig * call_v[rows, cols].astype(F32) - cpos_v[rows, cols].astype(F32)
+                jnp.tanh(0.5 * score) * call_v[rows, cols].astype(F32)
+                + cpos_v[rows, cols].astype(F32)
             ).astype(BF16)
 
         gsend_v[rows, :] = dot(st_v[rows, :], h_v[...]).astype(BF16)
@@ -273,37 +273,83 @@
             source, target, sems.at[0], sems.at[1], device_id=device, device_id_type=MESH
         ).start()
 
-    for o in range(1, ny + 1):
+    def beside(side, o):
+        if side == 0:
+            return over_x(o), lax.rem(my_x + o, nx)
+        return over_y(o), lax.rem(my_y + o, ny)
+
+    def piece(ref, side, at, rows, cols):
+        if side == 0:
+            return ref.at[:, at, rows[0], cols]
+        return ref.at[at, :, rows[1], cols]
+
+    def halves(width):
+        return pl.ds(0, width // 2), pl.ds(width // 2, width // 2)
+
+    def send_far(ref, side, rows, cols, far, sems):
+        _, at = beside(side, 2)
+        for way, o in ((0, 1), (1, 3)):
+            to, _ = beside(side, o)
+            send(piece(ref, side, at, rows, cols[way]), far.at[side, way], sems.at[side], to)
+
+    def send_near(ref, side, rows, cols, near, sems, way):
+        to, at = beside(side, 1 + 2 * way)
+        send(piece(ref, side, at, rows, cols[1 - way]), near.at[side, way], sems.at[2 + side], to)
+
+    def pass_on(ref, rows, cols, far, added, got, sems):
+        for side in range(2):
+            bytes_wait(far.at[side], sems.at[side, 1])
+            for way in range(2):
+                to, at = beside(side, 1 + 2 * way)
+                own = piece(ref, side, at, rows, cols[way])
+                for i in range(ny):
+                    added[side, way, i] = (
+                        own[i].astype(F32) + far[side, way, i].astype(F32)
+                    ).astype(BF16)
+                send(added.at[side, way], got.at[side, way], sems.at[4 + side], to)
+
+    def add_up(ref, rows, cols, near, got, middle, two, sems):
+        for side in range(2):
+            bytes_wait(near.at[side], sems.at[2 + side, 1])
+            bytes_wait(got.at[side], sems.at[4 + side, 1])
+            _, at = beside(side, 0)
+            for way in range(2):
+                own = piece(ref, side, at, rows, cols[way])
+                for i in range(ny):
+                    middle[side, i, :, cols[way]] = (
+                        own[i].astype(F32)
+                        + got[side, way, i].astype(F32)
+                        + near[side, 1 - way, i].astype(F32)
+                    ).astype(BF16)
+        for side in range(2):
+            for o in (2, 1, 3):
+                to, at = beside(1 - side, o)
+                send(middle.at[side, at], two.at[side, o - 1], sems.at[6 + side], to)
+
+    def drain(far, near, got, two, sems):
+        for side in range(2):
+            bytes_wait(far.at[side], sems.at[side, 0])
+            bytes_wait(near.at[side], sems.at[2 + side, 0])
+            bytes_wait(got.at[side], sems.at[4 + side, 0])
+            bytes_wait(two.at[side], sems.at[6 + side, 0])
+
+    head_rows = (low_rows, high_rows)
+    wide = halves(chan)
+    for o in (2, 1, 3, 0):
         y = lax.rem(my_y + o, ny)
         cols = pl.ds(pl.multiple_of(y * nx * span, nx * span), nx * span)
         terms = dot(st_v[:, cols], erecv_v[...], TN).astype(BF16)
         hsend_v[y] = terms.reshape(nx, span, chan)
-        if o < ny:
-            send(hsend_v.at[y, :, high_rows], hone_v.at[1, o - 1], h_sem.at[1], over_y(o))
-    for o in range(1, nx):
-        x = lax.rem(my_x + o, nx)
-        send(hsend_v.at[:, x, low_rows], hone_v.at[0, o - 1], h_sem.at[0], over_x(o))
-
-    bytes_wait(hone_v.at[1], h_sem.at[1, 1])
-    bytes_wait(hone_v.at[0], h_sem.at[0, 1])
+        if o == 2:
+            send_far(hsend_v, 1, head_rows, wide, hfar_v, h_sem)
+        elif o:
+            send_near(hsend_v, 1, head_rows, wide, hnear_v, h_sem, o // 2)
+    send_far(hsend_v, 0, head_rows, wide, hfar_v, h_sem)
+    for way in range(2):
+        send_near(hsend_v, 0, head_rows, wide, hnear_v, h_sem, way)
+
+    pass_on(hsend_v, head_rows, wide, hfar_v, hsum_v, hgot_v, h_sem)
     strip = 32
-
-    @pl.loop(0, ny)
-    def _(i):
-        for at in range(0, span // 2, strip):
-            part = pl.ds(at, strip)
-            total = hsend_v[i, my_x, part, :].astype(F32)
-            for o in range(nx - 1):
-                total = total + hone_v[0, o, i, part, :].astype(F32)
-            hmid_v[0, i, part, :] = total.astype(BF16)
-            total = hsend_v[my_y, i, pl.ds(span // 2 + at, strip), :].astype(F32)
-            for o in range(ny - 1):
-                total = total + hone_v[1, o, i, part, :].astype(F32)
-            hmid_v[1, i, part, :] = total.astype(BF16)
-
-    for o in range(1, ny):
-        send(hmid_v.at[0, lax.rem(my_y + o, ny)], htwo_v.at[0, o - 1], h_sem.at[2], over_y(o))
-        send(hmid_v.at[1, lax.rem(my_x + o, nx)], htwo_v.at[1, o - 1], h_sem.at[3], over_x(o))
 
     bytes_wait(grecv_v.at[pl.ds(0, (nl - 1) * cap)], g_sem.at[1])
     clip_grad = dot(d_v[...], grecv_v[...], TN) * (1.0 / 3.0)
@@ -323,95 +369,97 @@
         )
 
     part_rows = rows_dp // 2
-    low_part, high_part = pl.ds(0, part_rows), pl.ds(part_rows, part_rows)
+    conv_rows = (pl.ds(0, part_rows), pl.ds(part_rows, part_rows))
+    thin = halves(half)
 
     def spread(step):
         core_copy(step).wait_recv()
         both = (wown_v[step] + wrecv_v[step].astype(F32)).astype(BF16)
         dsend_v[step] = both.reshape(ny, nx, rows_dp, half)
-        for o in range(1, nx):
-            x = lax.rem(my_x + o, nx)
-            send(
-                dsend_v.at[step, :, x, low_part], done_v.at[step, 0, o - 1],
-                d_sem.at[step, 0], over_x(o),
-            )
-        for o in range(1, ny):
-            y = lax.rem(my_y + o, ny)
-            send(
-                dsend_v.at[step, y, :, high_part], done_v.at[step, 1, o - 1],
-                d_sem.at[step, 1], over_y(o),
-            )
+        for side in range(2):
+            send_far(dsend_v.at[step], side, conv_rows, thin, dfar_v.at[step], d_sem.at[step])
+        for side in range(2):
+            for way in range(2):
+                send_near(
+                    dsend_v.at[step], side, conv_rows, thin, dnear_v.at[step], d_sem.at[step], way
+                )
+
+    def carry(step):
+        pass_on(
+            dsend_v.at[step], conv_rows, thin, dfar_v.at[step], dsum_v.at[step],
+            dgot_v.at[step], d_sem.at[step],
+        )
 
     def respread(step):
-        bytes_wait(done_v.at[step, 0], d_sem.at[step, 0, 1])
-        total = dsend_v[step, :, my_x, low_part, :].astype(F32)
-        for o in range(nx - 1):
-            total = total + done_v[step, 0, o].astype(F32)
-        dmid_v[step, 0] = total.astype(BF16)
-        bytes_wait(done_v.at[step, 1], d_sem.at[step, 1, 1])
-        total = dsend_v[step, my_y, :, high_part, :].astype(F32)
-        for o in range(ny - 1):
-            total = total + done_v[step, 1, o].astype(F32)
-        dmid_v[step, 1] = total.astype(BF16)
-        for o in range(1, ny):
-            send(
-                dmid_v.at[step, 0, lax.rem(my_y + o, ny)], dtwo_v.at[step, 0, o - 1],
-                d_sem.at[step, 2], over_y(o),
-            )
-            send(
-                dmid_v.at[step, 1, lax.rem(my_x + o, nx)], dtwo_v.at[step, 1, o - 1],
-                d_sem.at[step, 3], over_x(o),
-            )
+        add_up(
+            dsend_v.at[step], conv_rows, thin, dnear_v.at[step], dgot_v.at[step],
+            dmid_v.at[step], dtwo_v.at[step], d_sem.at[step],
+        )
 
     def gather_step(step):
         for side, place in ((0, my_y), (1, my_x)):
-            bytes_wait(dtwo_v.at[step, side], d_sem.at[step, 2 + side, 1])
+            bytes_wait(dtwo_v.at[step, side], d_sem.at[step, 6 + side, 1])
             total = dmid_v[step, side, place].astype(F32)
             for o in range(ny - 1):
                 total = total + dtwo_v[step, side, o].astype(F32)
-            first = pl.multiple_of(step * rows_dp + side * part_rows, part_rows)
-            g_v[pl.ds(first, part_rows), :] = total
-
-    @pl.loop(0, 3)
-    def _(k):
+            g_v[pl.ds(step * rows_dp + side * part_rows, part_rows), :] = total
+
+    for k in range(3):
         left = jnp.concatenate([a1_v[3 * j + k] for j in range(3)], axis=0)
         leave(3 + k, dot(left, u1_v[...].reshape(3 * clips, chan), TN))
 
-    @pl.loop(0, 3)
-    def _(k):
-        taps = w_v[1, pl.ds(pl.multiple_of(k * chan, chan), chan), :]
+    for k in range(3):
+        taps = w_v[1, k * chan : (k + 1) * chan, :]
         for j in range(3):
             u0_v[3 * j + k] = (dot(u1_v[j], taps, NT) * sl0_v[3 * j + k]).astype(BF16)
 
-    @pl.loop(0, 3)
-    def _(k):
+    for k in range(3):
         spread(3 + k)
 
-    @pl.loop(0, 3)
-    def _(k):
+    for k in range(3):
         left = a_v[:, k].reshape(9 * clips, chan)
         leave(k, dot(left, u0_v[...].reshape(9 * clips, chan), TN))
-
-        @pl.when(k > 0)
-        def _():
+        if k == 0:
+            for step in (3, 4, 5):
+                carry(step)
+            add_up(hsend_v, head_rows, wide, hnear_v, hgot_v, hmid_v, htwo_v, h_sem)
+        else:
             spread(k - 1)
 
     spread(2)
+    carry(0)
+    carry(1)
 
     filled = 6 * rows_dp
     if g_v.shape[0] > filled:
         g_v[filled:, :] = jnp.zeros((g_v.shape[0] - filled, half), F32)
 
-    @pl.loop(0, 3)
-    def _(k):
-        respread(3 + k)
-
-    @pl.loop(0, 3)
-    def _(k):
-        respread(k)
+    for step in (3, 4, 5):
+        respread(step)
+    carry(2)
+    for step in range(3):
+        respread(step)
+
+    for step in (3, 4, 5, 0, 1, 2):
+        gather_step(step)
+
+    zsend_v[...] = g_v[...].T.astype(BF16).reshape(nl // 2, cols_leaf, g_v.shape[0])
+    for i in range(nl // 2):
+        to = core * (nl // 2) + i
+
+        @pl.when(to == me)
+        def _():
+            zrecv_v[my_z] = zsend_v[i]
+
+        @pl.when(to != me)
+        def _():
+            pltpu.make_async_remote_copy(
+                zsend_v.at[i], zrecv_v.at[my_z], zsend_sem.at[i], zrecv_sem.at[my_z],
+                device_id={"leaf": to}, device_id_type=MESH,
+            ).start()
 
     for side, place in ((0, my_y), (1, my_x)):
-        bytes_wait(htwo_v.at[side], h_sem.at[2 + side, 1])
+        bytes_wait(htwo_v.at[side], h_sem.at[6 + side, 1])
         for at in range(0, span // 2, strip):
             part = pl.ds(at, strip)
             total = hmid_v[side, place, part, :].astype(F32)
@@ -419,29 +467,6 @@
                 total = total + htwo_v[side, o, part, :].astype(F32)
             head_ref[pl.ds(side * (span // 2) + at, strip), :] = total.astype(BF16)
 
-    @pl.loop(0, 3)
-    def _(k):
-        gather_step(3 + k)
-
-    @pl.loop(0, 3)
-    def _(k):
-        gather_step(k)
-
-    zsend_v[...] = g_v[...].T.astype(BF16).reshape(nl // 2, cols_leaf, g_v.shape[0])
-    for i in range(nl // 2):
-        to = core * (nl // 2) + i
-
-        @pl.when(to == me)
-        def _():
-            zrecv_v[my_z] = zsend_v[i]
-
-        @pl.when(to != me)
-        def _():
-            pltpu.make_async_remote_copy(
-                zsend_v.at[i], zrecv_v.at[my_z], zsend_sem.at[i], zrecv_sem.at[my_z],
-                device_id={"leaf": to}, device_id_type=MESH,
-            ).start()
-
     giver = me // (nl // 2)
     zsum_v[...] = jnp.zeros(zsum_v.shape, F32)
     for z in range(nl // 2):
@@ -462,16 +487,12 @@
 
     bytes_wait(esend_v.at[pl.ds(0, (nl - 1) * cap)], e_sem.at[0])
     bytes_wait(gsend_v.at[pl.ds(0, (nl - 1) * cap)], g_sem.at[0])
-    for side in range(2):
-        bytes_wait(hone_v.at[side], h_sem.at[side, 0])
-        bytes_wait(htwo_v.at[side], h_sem.at[2 + side, 0])
+    drain(hfar_v, hnear_v, hgot_v, htwo_v, h_sem)
 
     @pl.loop(0, 6)
     def _(step):
         core_copy(step).wait_send()
-        for side in range(2):
-            bytes_wait(done_v.at[step, side], d_sem.at[step, side, 0])
-            bytes_wait(dtwo_v.at[step, side], d_sem.at[step, 2 + side, 0])
+        drain(dfar_v.at[step], dnear_v.at[step], dgot_v.at[step], dtwo_v.at[step], d_sem.at[step])
 
     for i in range(nl // 2):
 
@@ -531,7 +552,7 @@
         vm((slots, chan), BF16),
         vm((slots, chan), BF16),
         vm((ny, nx, span, chan), BF16),
-        vm((2, ny - 1, ny, span // 2, chan), BF16),
+        *[vm((2, 2, ny, span // 2, chan // 2), BF16) for _ in range(4)],
         vm((2, ny, span // 2, chan), BF16),
         vm((2, ny - 1, span // 2, chan), BF16),
         vm((3, clips, chan), BF16),
@@ -540,15 +561,15 @@
         vm((6, chan, half), BF16),
         vm((6, chan, half), BF16),
         vm((6, ny, nx, rows_dp, half), BF16),
-        vm((6, 2, ny - 1, ny, rows_dp // 2, half), BF16),
+        *[vm((6, 2, 2, ny, rows_dp // 2, half // 2), BF16) for _ in range(4)],
         vm((6, 2, ny, rows_dp // 2, half), BF16),
         vm((6, 2, ny - 1, rows_dp // 2, half), BF16),
         vm((filled, half), F32),
         vm((nl // 2, cols_leaf, filled), BF16),
         vm((nl // 2, cols_leaf, filled), BF16),
         vm((max(128, cols_leaf), filled), F32),
-        dma((3,)), dma((steps,)), dma((2,)), dma((1,)), dma((nl,)), dma((2,)), dma((4, 2)),
-        dma((6,)), dma((6,)), dma((6, 4, 2)), dma((nl // 2,)), dma((nl // 2,)),
+        dma((3,)), dma((steps,)), dma((2,)), dma((1,)), dma((nl,)), dma((2,)), dma((8, 2)),
+        dma((6,)), dma((6,)), dma((6, 8, 2)), dma((nl // 2,)), dma((nl // 2,)),
     ]
     whole = pl.BlockSpec(memory_space=pltpu.VMEM)
     far = pl.BlockSpec(memory_space=pl.ANY)

time: 85.6 us -> 85.9 us (level)
  no operation moved by 1% of the time
where the time goes in v4:
time: 85.9 us; the launch traced here: 85.7 us
  Pallas kernels  85.1 us (99%)
    pallas_call x1, Pallas kernels, body(): pl.pallas_call(functools.partial(kernel, ny, nx, nl, chunk), out_shape=(j...  83.5 us

profile of v4, /device:TPU:1, one launch (start us, length us, event | category | flops | bytes accessed | tf_op | source)
XLA Modules:
  0.0 85.7 jit_solution(2121263979412076736)
XLA Ops:
  0.6 83.5 %shard_map.68 = (bf16[2,3,32,32]{3,2,1,0:T(8,128)(2,1)}, bf16[128,512]{1,0:T(8,128)(2,1)}) custom-call(bf16[9,3,192,512]{3,2,1,0:T(8,128)(2,1)} %bitcast.6, bf16[2,1536,512]{2,1,0:T(8,128)(2,1)} %bitcast.7, bf16[2048,512]{1,0:T(8,128)(2,1)} %h_hbm.1, s32[2,192]{1,0:T(2,128)} %bitcast.9, s32[2,8,192]{2,1,0:T(8,128)} %bitcast.8), custom_call_target="tpu_custom_call" | custom-call | tf_op jit(solution)/shard_map/pallas_call | solution.py:576
  84.1 1.6 %shard_map.69 = (bf16[2,3,32,32]{3,2,1,0:T(8,128)(2,1)}, bf16[128,512]{1,0:T(8,128)(2,1)}) custom-call(bf16[2,3,32,32]{3,2,1,0:T(8,128)(2,1)} %get-tuple-element.4.conv_ref, bf16[128,512]{1,0:T(8,128)(2,1)} %get-tuple-element.5.head_ref), custom_call_target="tpu_custom_call" | custom-call | tf_op jit(solution)/shard_map/pallas_call | solution.py:589

commit v5 on v3

--- a/solution.py
+++ b/solution.py
@@ -96,29 +96,24 @@
         < lax.broadcasted_iota(jnp.int32, (clips, clips), 1)
     ).astype(F32).astype(BF16)
     slot_iota = lax.broadcasted_iota(jnp.int32, (slots, clips), 0)
-    list_iota = lax.broadcasted_iota(jnp.int32, (nl * 128, clips), 0)
     base = jnp.zeros((nl, 1), F32)
     spots = []
-    lists = jnp.zeros((2 * pairs, nl * 128), F32)
+    lists = jnp.zeros((2 * pairs, slots), F32)
     for r in range(2):
         hit = (own_ref[r : r + 1, :] == owner_iota).astype(F32)
         rank = dot(hit.astype(BF16), before) + base
         base = base + jnp.sum(hit, axis=1, keepdims=True)
 
-        def place(stride):
-            spot = jnp.sum(
-                hit * (rank + (owner_iota * stride).astype(F32)), axis=0, keepdims=True
-            )
-            return spot.astype(jnp.int32)
-
-        spots.append((slot_iota == place(cap)).astype(F32).astype(BF16))
-        wide = (list_iota == place(128)).astype(F32).astype(BF16)
+        place = jnp.sum(hit * (rank + (owner_iota * cap).astype(F32)), axis=0, keepdims=True)
+        spots.append((slot_iota == place.astype(jnp.int32)).astype(F32).astype(BF16))
         ident = node_ref[r] + 1
         parts = jnp.concatenate([ident >> 7, ident & 127], axis=0).astype(F32).astype(BF16)
-        lists = lists + dot(parts, wide, NT)
+        lists = lists + dot(parts, spots[r], NT)
     d_v[...] = spots[0] + spots[1]
+    blank = jnp.zeros((2 * pairs, 128 - cap), F32)
     for o in range(nl):
-        nsend_v[o] = lists[:, o * 128 : (o + 1) * 128].astype(BF16)
+        listed = jnp.concatenate([lists[:, o * cap : (o + 1) * cap], blank], axis=1)
+        nsend_v[o] = listed.astype(BF16)
 
     def block(i):
         return pl.ds(pl.multiple_of(i * cap, cap), cap)
@@ -180,7 +175,7 @@
             folded = jnp.concatenate([a1_v[3 * j + k] for k in range(3)], axis=1)
             sl1_v[j, :, cols] = dot(folded, w_v[1, :, cols])
 
-        @pl.loop(0, steps)
+        @pl.loop(0, steps, unroll=True)
         def _(i):
             part = pl.ds(pl.multiple_of(i * chunk, chunk), chunk)
             total = jnp.zeros((chunk, half), F32)
@@ -228,8 +223,9 @@
                 ident = named[i * 16 : (i + 1) * 16, q : q + 1]
                 tally = tally + jnp.where(ident == node_iota, weight, 0.0)
             positive = jnp.floor(tally * (1.0 / 16.0))
-            cpos_v[part, :] = positive.astype(BF16)
-            call_v[part, :] = (tally - 16.0 * positive).astype(BF16)
+            every = 0.5 * tally - 8.0 * positive
+            call_v[part, :] = every.astype(BF16)
+            cpos_v[part, :] = (every - positive).astype(BF16)
 
     lanes = nodes // 4
     for t in range(nl // per):
@@ -242,13 +238,12 @@
         rows = pl.ds(t * per * cap, per * cap)
         emb = erecv_v[rows, :]
 
-        @pl.loop(0, 4)
-        def _(n):
-            cols = pl.ds(pl.multiple_of(n * lanes, lanes), lanes)
+        for n in range(4):
+            cols = pl.ds(n * lanes, lanes)
             score = dot(emb, ht_v[:, cols])
-            sig = 0.5 * jnp.tanh(0.5 * score) + 0.5
             st_v[rows, cols] = (
-                sig * call_v[rows, cols].astype(F32) - cpos_v[rows, cols].astype(F32)
+                jnp.tanh(0.5 * score) * call_v[rows, cols].astype(F32)
+                + cpos_v[rows, cols].astype(F32)
             ).astype(BF16)
 
         gsend_v[rows, :] = dot(st_v[rows, :], h_v[...]).astype(BF16)
@@ -284,26 +279,27 @@
         x = lax.rem(my_x + o, nx)
         send(hsend_v.at[:, x, low_rows], hone_v.at[0, o - 1], h_sem.at[0], over_x(o))
 
-    bytes_wait(hone_v.at[1], h_sem.at[1, 1])
-    bytes_wait(hone_v.at[0], h_sem.at[0, 1])
     strip = 32
 
-    @pl.loop(0, ny)
-    def _(i):
-        for at in range(0, span // 2, strip):
-            part = pl.ds(at, strip)
-            total = hsend_v[i, my_x, part, :].astype(F32)
-            for o in range(nx - 1):
-                total = total + hone_v[0, o, i, part, :].astype(F32)
-            hmid_v[0, i, part, :] = total.astype(BF16)
-            total = hsend_v[my_y, i, pl.ds(span // 2 + at, strip), :].astype(F32)
-            for o in range(ny - 1):
-                total = total + hone_v[1, o, i, part, :].astype(F32)
-            hmid_v[1, i, part, :] = total.astype(BF16)
-
-    for o in range(1, ny):
-        send(hmid_v.at[0, lax.rem(my_y + o, ny)], htwo_v.at[0, o - 1], h_sem.at[2], over_y(o))
-        send(hmid_v.at[1, lax.rem(my_x + o, nx)], htwo_v.at[1, o - 1], h_sem.at[3], over_x(o))
+    def head_middle():
+        bytes_wait(hone_v.at[1], h_sem.at[1, 1])
+        bytes_wait(hone_v.at[0], h_sem.at[0, 1])
+        @pl.loop(0, ny)
+        def _(i):
+            for at in range(0, span // 2, strip):
+                part = pl.ds(at, strip)
+                total = hsend_v[i, my_x, part, :].astype(F32)
+                for o in range(nx - 1):
+                    total = total + hone_v[0, o, i, part, :].astype(F32)
+                hmid_v[0, i, part, :] = total.astype(BF16)
+                total = hsend_v[my_y, i, pl.ds(span // 2 + at, strip), :].astype(F32)
+                for o in range(ny - 1):
+                    total = total + hone_v[1, o, i, part, :].astype(F32)
+                hmid_v[1, i, part, :] = total.astype(BF16)
+
+        for o in range(1, ny):
+            send(hmid_v.at[0, lax.rem(my_y + o, ny)], htwo_v.at[0, o - 1], h_sem.at[2], over_y(o))
+            send(hmid_v.at[1, lax.rem(my_x + o, nx)], htwo_v.at[1, o - 1], h_sem.at[3], over_x(o))
 
     bytes_wait(grecv_v.at[pl.ds(0, (nl - 1) * cap)], g_sem.at[1])
     clip_grad = dot(d_v[...], grecv_v[...], TN) * (1.0 / 3.0)
@@ -325,17 +321,20 @@
     part_rows = rows_dp // 2
     low_part, high_part = pl.ds(0, part_rows), pl.ds(part_rows, part_rows)
 
+    def far_first(n):
+        return sorted(range(1, n), key=lambda o: -min(o, n - o))
+
     def spread(step):
         core_copy(step).wait_recv()
         both = (wown_v[step] + wrecv_v[step].astype(F32)).astype(BF16)
         dsend_v[step] = both.reshape(ny, nx, rows_dp, half)
-        for o in range(1, nx):
+        for o in far_first(nx):
             x = lax.rem(my_x + o, nx)
             send(
                 dsend_v.at[step, :, x, low_part], done_v.at[step, 0, o - 1],
                 d_sem.at[step, 0], over_x(o),
             )
-        for o in range(1, ny):
+        for o in far_first(ny):
             y = lax.rem(my_y + o, ny)
             send(
                 dsend_v.at[step, y, :, high_part], done_v.at[step, 1, o - 1],
@@ -369,31 +368,24 @@
             total = dmid_v[step, side, place].astype(F32)
             for o in range(ny - 1):
                 total = total + dtwo_v[step, side, o].astype(F32)
-            first = pl.multiple_of(step * rows_dp + side * part_rows, part_rows)
-            g_v[pl.ds(first, part_rows), :] = total
-
-    @pl.loop(0, 3)
-    def _(k):
+            g_v[pl.ds(step * rows_dp + side * part_rows, part_rows), :] = total
+
+    for k in range(3):
         left = jnp.concatenate([a1_v[3 * j + k] for j in range(3)], axis=0)
         leave(3 + k, dot(left, u1_v[...].reshape(3 * clips, chan), TN))
 
-    @pl.loop(0, 3)
-    def _(k):
-        taps = w_v[1, pl.ds(pl.multiple_of(k * chan, chan), chan), :]
+    for k in range(3):
+        taps = w_v[1, k * chan : (k + 1) * chan, :]
         for j in range(3):
             u0_v[3 * j + k] = (dot(u1_v[j], taps, NT) * sl0_v[3 * j + k]).astype(BF16)
-
-    @pl.loop(0, 3)
-    def _(k):
         spread(3 + k)
 
-    @pl.loop(0, 3)
-    def _(k):
+    for k in range(3):
         left = a_v[:, k].reshape(9 * clips, chan)
         leave(k, dot(left, u0_v[...].reshape(9 * clips, chan), TN))
-
-        @pl.when(k > 0)
-        def _():
+        if k == 0:
+            head_middle()
+        else:
             spread(k - 1)
 
     spread(2)
@@ -402,13 +394,26 @@
     if g_v.shape[0] > filled:
         g_v[filled:, :] = jnp.zeros((g_v.shape[0] - filled, half), F32)
 
-    @pl.loop(0, 3)
-    def _(k):
-        respread(3 + k)
-
-    @pl.loop(0, 3)
-    def _(k):
-        respread(k)
+    for step in (3, 4, 5, 0, 1, 2):
+        respread(step)
+
+    for step in (3, 4, 5, 0, 1, 2):
+        gather_step(step)
+
+    zsend_v[...] = g_v[...].T.astype(BF16).reshape(nl // 2, cols_leaf, g_v.shape[0])
+    for i in range(nl // 2):
+        to = core * (nl // 2) + i
+
+        @pl.when(to == me)
+        def _():
+            zrecv_v[my_z] = zsend_v[i]
+
+        @pl.when(to != me)
+        def _():
+            pltpu.make_async_remote_copy(
+                zsend_v.at[i], zrecv_v.at[my_z], zsend_sem.at[i], zrecv_sem.at[my_z],
+                device_id={"leaf": to}, device_id_type=MESH,
+            ).start()
 
     for side, place in ((0, my_y), (1, my_x)):
         bytes_wait(htwo_v.at[side], h_sem.at[2 + side, 1])
@@ -418,29 +423,6 @@
             for o in range(ny - 1):
                 total = total + htwo_v[side, o, part, :].astype(F32)
             head_ref[pl.ds(side * (span // 2) + at, strip), :] = total.astype(BF16)
-
-    @pl.loop(0, 3)
-    def _(k):
-        gather_step(3 + k)
-
-    @pl.loop(0, 3)
-    def _(k):
-        gather_step(k)
-
-    zsend_v[...] = g_v[...].T.astype(BF16).reshape(nl // 2, cols_leaf, g_v.shape[0])
-    for i in range(nl // 2):
-        to = core * (nl // 2) + i
-
-        @pl.when(to == me)
-        def _():
-            zrecv_v[my_z] = zsend_v[i]
-
-        @pl.when(to != me)
-        def _():
-            pltpu.make_async_remote_copy(
-                zsend_v.at[i], zrecv_v.at[my_z], zsend_sem.at[i], zrecv_sem.at[my_z],
-                device_id={"leaf": to}, device_id_type=MESH,
-            ).start()
 
     giver = me // (nl // 2)
     zsum_v[...] = jnp.zeros(zsum_v.shape, F32)

time: 85.6 us -> 83.2 us (0.972)
  Pallas kernels: 84.8 us -> 82.4 us
    pallas_call x1, Pallas kernels: 83.2 us -> 80.8 us  [body(): pl.pallas_call(functools.partial(kernel, ny, nx, nl, chunk), out_shape=(j...]
where the time goes in v5:
time: 83.2 us; the launch traced here: 83 us
  Pallas kernels  82.4 us (99%)
    pallas_call x1, Pallas kernels, body(): pl.pallas_call(functools.partial(kernel, ny, nx, nl, chunk), out_shape=(j...  80.8 us

profile of v5, /device:TPU:1, one launch (start us, length us, event | category | flops | bytes accessed | tf_op | source)
XLA Modules:
  0.0 83.0 jit_solution(7903620367149387820)
XLA Ops:
  0.6 80.8 %shard_map.68 = (bf16[2,3,32,32]{3,2,1,0:T(8,128)(2,1)}, bf16[128,512]{1,0:T(8,128)(2,1)}) custom-call(bf16[9,3,192,512]{3,2,1,0:T(8,128)(2,1)} %bitcast.6, bf16[2,1536,512]{2,1,0:T(8,128)(2,1)} %bitcast.7, bf16[2048,512]{1,0:T(8,128)(2,1)} %h_hbm.1, s32[2,192]{1,0:T(2,128)} %bitcast.9, s32[2,8,192]{2,1,0:T(8,128)} %bitcast.8), custom_call_target="tpu_custom_call" | custom-call | tf_op jit(solution)/shard_map/pallas_call | solution.py:537
  81.4 1.6 %shard_map.69 = (bf16[2,3,32,32]{3,2,1,0:T(8,128)(2,1)}, bf16[128,512]{1,0:T(8,128)(2,1)}) custom-call(bf16[2,3,32,32]{3,2,1,0:T(8,128)(2,1)} %get-tuple-element.4.conv_ref, bf16[128,512]{1,0:T(8,128)(2,1)} %get-tuple-element.5.head_ref), custom_call_target="tpu_custom_call" | custom-call | tf_op jit(solution)/shard_map/pallas_call | solution.py:550

commit v6 on v5

--- a/solution.py
+++ b/solution.py
@@ -383,12 +383,11 @@
     for k in range(3):
         left = a_v[:, k].reshape(9 * clips, chan)
         leave(k, dot(left, u0_v[...].reshape(9 * clips, chan), TN))
-        if k == 0:
-            head_middle()
-        else:
+        if k > 0:
             spread(k - 1)
 
     spread(2)
+    head_middle()
 
     filled = 6 * rows_dp
     if g_v.shape[0] > filled:

time: 83.2 us -> 81.4 us (0.978)
  Pallas kernels: 82.4 us -> 80.6 us
    pallas_call x1, Pallas kernels: 80.8 us -> 79 us  [body(): pl.pallas_call(functools.partial(kernel, ny, nx, nl, chunk), out_shape=(j...]
where the time goes in v6:
time: 81.4 us; the launch traced here: 81.2 us
  Pallas kernels  80.6 us (99%)
    pallas_call x1, Pallas kernels, body(): pl.pallas_call(functools.partial(kernel, ny, nx, nl, chunk), out_shape=(j...  79 us

profile of v6, /device:TPU:1, one launch (start us, length us, event | category | flops | bytes accessed | tf_op | source)
XLA Modules:
  0.0 81.2 jit_solution(8743599208798702016)
XLA Ops:
  0.6 79.0 %shard_map.68 = (bf16[2,3,32,32]{3,2,1,0:T(8,128)(2,1)}, bf16[128,512]{1,0:T(8,128)(2,1)}) custom-call(bf16[9,3,192,512]{3,2,1,0:T(8,128)(2,1)} %bitcast.6, bf16[2,1536,512]{2,1,0:T(8,128)(2,1)} %bitcast.7, bf16[2048,512]{1,0:T(8,128)(2,1)} %h_hbm.1, s32[2,192]{1,0:T(2,128)} %bitcast.9, s32[2,8,192]{2,1,0:T(8,128)} %bitcast.8), custom_call_target="tpu_custom_call" | custom-call | tf_op jit(solution)/shard_map/pallas_call | solution.py:536
  79.6 1.6 %shard_map.69 = (bf16[2,3,32,32]{3,2,1,0:T(8,128)(2,1)}, bf16[128,512]{1,0:T(8,128)(2,1)}) custom-call(bf16[2,3,32,32]{3,2,1,0:T(8,128)(2,1)} %get-tuple-element.4.conv_ref, bf16[128,512]{1,0:T(8,128)(2,1)} %get-tuple-element.5.head_ref), custom_call_target="tpu_custom_call" | custom-call | tf_op jit(solution)/shard_map/pallas_call | solution.py:549
